TPU v7x, 512 devices: a whole 4x8x8 slice. The times are simulated.
512 devices in a mesh: row: 16 (over y, core), col: 32 (over z, x).
Axes of the slice: x: 4, y: 8, z: 8, core: 2. Of those that a mesh axis runs over, the one named last changes fastest.
Arguments:
- initial: float32 [16, 64, 64, 576], P('row', 'col'), as said below
- pattern: int32 [16, 64, 9], P('row', 'col'), may hold values from 0 to 1, as said below
- branch: int32 [5], replicated, may hold values from 0 to 1, as said below
Outputs:
- density: float32 [16, 64, 64, 576], P('row', 'col')
- occupation: float32 [5], replicated
Inputs may be any that keep to these rules, and one draw needn't show every extreme that they name: pattern[a, b, 4] is 1 for every atom, and pattern[a, b, k] equals pattern[(a + da) mod 16, (b + db) mod 64, 8 - k] with (da, db) = (k // 3 - 1, k % 3 - 1). The block matrix is symmetric: the block of initial at atom ((a + da) mod 16, (b + db) mod 64) and offset 8 - k is the transpose of its block at atom (a, b) and offset k. branch[0] and branch[1] differ.
All inputs are finite; a program needn't handle non-finite values.
Results may differ from a plain program's by a relative error of at most 0.0003.
Values sent between devices are 32-bit elements; how exact they have to be, the bound alone decides.
A program may use at most 64 MiB of HBM per device.

v0:
```python
from functools import reduce

import jax
import jax.numpy as jnp
from jax import lax
from jax.sharding import PartitionSpec as P

ITERS = 5


def padded(cells, sides, width):
    for axis, dim in sides:
        count = lax.axis_size(axis)
        head = lax.slice_in_dim(cells, 0, width, axis=dim)
        tail = lax.slice_in_dim(cells, cells.shape[dim] - width, cells.shape[dim], axis=dim)
        cells = jnp.concatenate(
            [
                lax.ppermute(tail, axis, [(i, (i + 1) % count) for i in range(count)]),
                cells,
                lax.ppermute(head, axis, [((i + 1) % count, i) for i in range(count)]),
            ],
            axis=dim,
        )
    return cells


def offset_of(position):
    return (position // 3 - 1, position % 3 - 1)


def square_blocks(extended, row_count, col_count):
    block_size = extended.shape[2]
    center = extended[1 : row_count + 1, 1 : col_count + 1]
    split_view = extended.reshape(row_count + 2, col_count + 2, block_size, 3, 3 * block_size)
    partial_terms = [[] for position in range(9)]
    for source in range(9):
        step_a, step_b = offset_of(source)
        left_block = center[:, :, :, source * block_size : (source + 1) * block_size]
        neighbour = split_view[
            1 + step_a : 1 + step_a + row_count, 1 + step_b : 1 + step_b + col_count
        ]
        lowest = max(-1, -1 - step_b)
        highest = min(1, 1 - step_b)
        for reach_a in (-1, 0, 1):
            target_a = step_a + reach_a
            if abs(target_a) > 1:
                continue
            right_block = neighbour[
                :, :, :, reach_a + 1, (lowest + 1) * block_size : (highest + 2) * block_size
            ]
            product = jnp.einsum(
                "abrk,abkx->abrx",
                left_block,
                right_block,
                precision=lax.Precision.HIGHEST,
                preferred_element_type=jnp.float32,
            )
            for reach_b in range(lowest, highest + 1):
                target = (target_a + 1) * 3 + (step_b + reach_b + 1)
                column_start = (reach_b - lowest) * block_size
                partial_terms[target].append(product[..., column_start : column_start + block_size])
    return jnp.concatenate([reduce(jnp.add, terms) for terms in partial_terms], axis=-1)


def surround(current):
    return padded(current, (("row", 0), ("col", 1)), 1)


def on_device(initial, pattern, branch):
    row_count, col_count, block_size = (initial.shape[0], initial.shape[1], initial.shape[2])
    mask = jnp.repeat(pattern.astype(jnp.float32), block_size, axis=2)[:, :, None, :]
    current = initial * mask
    matrix_order = row_count * col_count * block_size * lax.axis_size("row") * lax.axis_size("col")
    occupations = []
    for iteration in range(ITERS):
        extended = surround(current)
        square = square_blocks(extended, row_count, col_count)
        updated = jnp.where(branch[iteration] == 0, square, 2.0 * current - square)
        current = updated * mask
        local_sum = jnp.sum(
            jnp.trace(current[..., 4 * block_size : 5 * block_size], axis1=2, axis2=3)
        )
        occupations.append(lax.psum(local_sum, ("row", "col")) / matrix_order)
    occupation = jnp.stack(occupations)
    return (current, occupation)


def solution(mesh):
    return jax.shard_map(
        on_device,
        mesh=mesh,
        in_specs=(P("row", "col", None, None), P("row", "col", None), P()),
        out_specs=(P("row", "col", None, None), P()),
        check_vma=False,
    )
```

profile of v0, /device:TPU:1, one launch (start us, length us, event | category | flops | bytes accessed | tf_op | source)
XLA Modules:
  0.0 324.9 jit_solution(1757417325132412761)
XLA Ops:
  5.2 4.2 %collective-permute-start.1 = (f32[1,2,64,576]{3,2,1,0:T(8,128)S(1)}, f32[1,2,64,576]{3,2,1,0:T(8,128)S(1)}, u32[]{:S(2)}, u32[]{:S(2)}) collective-permute-start(f32[1,2,64,576]{3,2,1,0:T(8,128)S(1)} %broadcast_multiply_fusion), channel_id=1, source_target_pairs={{32,0},{64,32},{96,64},{128,96},{160,128},{192,160},{224,192},{256... | collective-permute-start | bytes 884744 | tf_op jit(solution)/shard_map/ppermute | solution.py:20
  11.8 3.1 collective-permute-start.2
  15.0 11.7 %collective-permute-start.3 = (f32[3,1,64,576]{3,2,1,0:T(8,128)S(1)}, f32[3,1,64,576]{3,2,1,0:T(8,128)S(1)}, u32[]{:S(2)}, u32[]{:S(2)}) collective-permute-start(f32[3,1,64,576]{3,2,1,0:T(8,128)S(1)} %get-tuple-element.126), channel_id=1, source_target_pairs={{1,0},{2,1},{3,2},{4,3},{5,4},{6,5},{7,6},{8,7},{9,8},{10,9},{11,1... | collective-permute-start | bytes 1327112 | tf_op jit(solution)/shard_map/ppermute | solution.py:20
  27.9 8.3 %collective-permute-done.2 = f32[3,1,64,576]{3,2,1,0:T(8,128)S(1)} collective-permute-done((f32[3,1,64,576]{3,2,1,0:T(8,128)S(1)}, f32[3,1,64,576]{3,2,1,0:T(8,128)S(1)}, u32[]{:S(2)}, u32[]{:S(2)}) %collective-permute-start.2) | collective-permute-done | bytes 442400 | tf_op jit(solution)/shard_map/ppermute | solution.py:18
  38.7 3.3 %reshape.756 = f32[3,4,64,3,192]{4,3,2,1,0:T(4,128)S(1)} reshape(f32[3,4,64,576]{3,2,1,0:T(8,128)} %pad_maximum_fusion) | data formatting | bytes 3538944 | tf_op jit(solution)/shard_map/reshape | solution.py:34
  51.3 3.8 %collective-permute-done.4 = f32[1,2,64,576]{3,2,1,0:T(8,128)S(1)} collective-permute-done((f32[1,2,64,576]{3,2,1,0:T(8,128)S(1)}, f32[1,2,64,576]{3,2,1,0:T(8,128)S(1)}, u32[]{:S(2)}, u32[]{:S(2)}) %collective-permute-start.4) | collective-permute-done | bytes 294944 | tf_op jit(solution)/shard_map/ppermute | solution.py:18
  55.1 2.8 collective-permute-done.5
  59.9 7.6 %collective-permute-start.7 = (f32[3,1,64,576]{3,2,1,0:T(8,128)S(1)}, f32[3,1,64,576]{3,2,1,0:T(8,128)S(1)}, u32[]{:S(2)}, u32[]{:S(2)}) collective-permute-start(f32[3,1,64,576]{3,2,1,0:T(8,128)S(1)} %get-tuple-element.124), channel_id=1, source_target_pairs={{1,0},{2,1},{3,2},{4,3},{5,4},{6,5},{7,6},{8,7},{9,8},{10,9},{11,1... | collective-permute-start | bytes 1327112 | tf_op jit(solution)/shard_map/ppermute | solution.py:20
  68.3 7.6 %collective-permute-done.6 = f32[3,1,64,576]{3,2,1,0:T(8,128)S(1)} collective-permute-done((f32[3,1,64,576]{3,2,1,0:T(8,128)S(1)}, f32[3,1,64,576]{3,2,1,0:T(8,128)S(1)}, u32[]{:S(2)}, u32[]{:S(2)}) %collective-permute-start.6) | collective-permute-done | bytes 442400 | tf_op jit(solution)/shard_map/ppermute | solution.py:18
  78.2 3.3 %reshape.787 = f32[3,4,64,3,192]{4,3,2,1,0:T(4,128)S(1)} reshape(f32[3,4,64,576]{3,2,1,0:T(8,128)} %pad_maximum_fusion.1) | data formatting | bytes 3538944 | tf_op jit(solution)/shard_map/reshape | solution.py:34
  91.8 3.5 %collective-permute-done.8 = f32[1,2,64,576]{3,2,1,0:T(8,128)S(1)} collective-permute-done((f32[1,2,64,576]{3,2,1,0:T(8,128)S(1)}, f32[1,2,64,576]{3,2,1,0:T(8,128)S(1)}, u32[]{:S(2)}, u32[]{:S(2)}) %collective-permute-start.8) | collective-permute-done | bytes 294944 | tf_op jit(solution)/shard_map/ppermute | solution.py:18
  95.3 2.8 collective-permute-done.9
  100.2 7.7 %collective-permute-start.11 = (f32[3,1,64,576]{3,2,1,0:T(8,128)S(1)}, f32[3,1,64,576]{3,2,1,0:T(8,128)S(1)}, u32[]{:S(2)}, u32[]{:S(2)}) collective-permute-start(f32[3,1,64,576]{3,2,1,0:T(8,128)S(1)} %get-tuple-element.122), channel_id=1, source_target_pairs={{1,0},{2,1},{3,2},{4,3},{5,4},{6,5},{7,6},{8,7},{9,8},{10,9},{11,1... | collective-permute-start | bytes 1327112 | tf_op jit(solution)/shard_map/ppermute | solution.py:20
  108.5 7.3 %collective-permute-done.10 = f32[3,1,64,576]{3,2,1,0:T(8,128)S(1)} collective-permute-done((f32[3,1,64,576]{3,2,1,0:T(8,128)S(1)}, f32[3,1,64,576]{3,2,1,0:T(8,128)S(1)}, u32[]{:S(2)}, u32[]{:S(2)}) %collective-permute-start.10) | collective-permute-done | bytes 442400 | tf_op jit(solution)/shard_map/ppermute | solution.py:18
  116.8 2.9 reshape.818
  119.7 4.2 %fusion.34 = (f32[1,2,64,1,128]{4,3,2,1,0:T(1,128)S(1)}, f32[1,2,64,1,128]{4,3,2,1,0:T(1,128)S(1)}, f32[1,2,64,1,128]{4,3,2,1,0:T(1,128)S(1)}, f32[1,2,64,1,128]...) fusion(f32[3,4,64,3,192]{4,3,2,1,0:T(4,128)} %reshape.818), kind=kLoop, calls=%fused_computation.438 | loop fusion | bytes 1835008 | tf_op jit(solution)/shard_map/slice | solution.py:48
  123.8 2.9 fusion.35
  135.3 3.2 collective-permute-done.12
  138.5 2.8 collective-permute-done.13
  143.3 7.7 %collective-permute-start.15 = (f32[3,1,64,576]{3,2,1,0:T(8,128)S(1)}, f32[3,1,64,576]{3,2,1,0:T(8,128)S(1)}, u32[]{:S(2)}, u32[]{:S(2)}) collective-permute-start(f32[3,1,64,576]{3,2,1,0:T(8,128)S(1)} %get-tuple-element.120), channel_id=1, source_target_pairs={{1,0},{2,1},{3,2},{4,3},{5,4},{6,5},{7,6},{8,7},{9,8},{10,9},{11,1... | collective-permute-start | bytes 1327112 | tf_op jit(solution)/shard_map/ppermute | solution.py:20
  151.6 7.1 %collective-permute-done.14 = f32[3,1,64,576]{3,2,1,0:T(8,128)S(1)} collective-permute-done((f32[3,1,64,576]{3,2,1,0:T(8,128)S(1)}, f32[3,1,64,576]{3,2,1,0:T(8,128)S(1)}, u32[]{:S(2)}, u32[]{:S(2)}) %collective-permute-start.14) | collective-permute-done | bytes 442400 | tf_op jit(solution)/shard_map/ppermute | solution.py:18
  159.7 2.9 reshape.849
  162.6 4.2 %fusion.32 = (f32[1,2,64,1,128]{4,3,2,1,0:T(1,128)S(1)}, f32[1,2,64,1,128]{4,3,2,1,0:T(1,128)S(1)}, f32[1,2,64,1,128]{4,3,2,1,0:T(1,128)S(1)}, f32[1,2,64,1,128]...) fusion(f32[3,4,64,3,192]{4,3,2,1,0:T(4,128)} %reshape.849), kind=kLoop, calls=%fused_computation.436 | loop fusion | bytes 1835008 | tf_op jit(solution)/shard_map/slice | solution.py:48
  166.8 2.9 fusion.33
  178.4 3.2 collective-permute-done.16
  181.6 2.8 collective-permute-done.17
  186.5 7.7 %collective-permute-start.19 = (f32[3,1,64,576]{3,2,1,0:T(8,128)S(1)}, f32[3,1,64,576]{3,2,1,0:T(8,128)S(1)}, u32[]{:S(2)}, u32[]{:S(2)}) collective-permute-start(f32[3,1,64,576]{3,2,1,0:T(8,128)S(1)} %get-tuple-element.118), channel_id=1, source_target_pairs={{1,0},{2,1},{3,2},{4,3},{5,4},{6,5},{7,6},{8,7},{9,8},{10,9},{11,1... | collective-permute-start | bytes 1327112 | tf_op jit(solution)/shard_map/ppermute | solution.py:20
  194.9 6.9 %collective-permute-done.18 = f32[3,1,64,576]{3,2,1,0:T(8,128)S(1)} collective-permute-done((f32[3,1,64,576]{3,2,1,0:T(8,128)S(1)}, f32[3,1,64,576]{3,2,1,0:T(8,128)S(1)}, u32[]{:S(2)}, u32[]{:S(2)}) %collective-permute-start.18) | collective-permute-done | bytes 442400 | tf_op jit(solution)/shard_map/ppermute | solution.py:18
  202.9 2.9 reshape.880
  205.7 4.2 %fusion.30 = (f32[1,2,64,1,128]{4,3,2,1,0:T(1,128)S(1)}, f32[1,2,64,1,128]{4,3,2,1,0:T(1,128)S(1)}, f32[1,2,64,1,128]{4,3,2,1,0:T(1,128)S(1)}, f32[1,2,64,1,128]...) fusion(f32[3,4,64,3,192]{4,3,2,1,0:T(4,128)} %reshape.880), kind=kLoop, calls=%fused_computation.434 | loop fusion | bytes 1835008 | tf_op jit(solution)/shard_map/slice | solution.py:48
  209.9 2.9 fusion.31
  219.7 101.5 %all-reduce = (f32[]{:T(128)}, f32[]{:T(128)}, f32[]{:T(128)}, f32[]{:T(128)}, f32[]{:T(128)}) all-reduce(f32[]{:T(128)} %get-tuple-element.6, f32[]{:T(128)} %get-tuple-element.3, f32[]{:T(128)} %get-tuple-element.4, f32[]{:T(128)} %get-tuple-element.5, f32[]{:T(128)} %get-tuple-element.2), channel_id=1, replica_groups=mesh['row'=16,'col'=32] {'row','col'}, use_global_device_ids=true, to_apply=%region_1.2 | all-reduce | flops 5 | bytes 40 | tf_op jit(solution)/shard_map/psum | solution.py:83
  (188 shorter events, 67.1 us)
Async XLA Ops:
  2.5 24.2 %copy-start.2 = (s32[5]{0:T(128)S(1)}, s32[5]{0:T(128)}, u32[]{:S(2)}) copy-start(s32[5]{0:T(128)} %param.5) | copy-start | bytes 64
  2.5 8.0 %collective-permute-start = (f32[1,2,64,576]{3,2,1,0:T(8,128)S(1)}, f32[1,2,64,576]{3,2,1,0:T(8,128)S(1)}, u32[]{:S(2)}, u32[]{:S(2)}) collective-permute-start(f32[1,2,64,576]{3,2,1,0:T(8,128)S(1)} %broadcast_multiply_fusion), channel_id=1, source_target_pairs={{0,32},{32,64},{64,96},{96,128},{128,160},{160,192},{192,224},{224... | collective-permute-start | bytes 884744 | tf_op jit(solution)/shard_map/ppermute | solution.py:18
  5.2 6.5 %collective-permute-start.1 = (f32[1,2,64,576]{3,2,1,0:T(8,128)S(1)}, f32[1,2,64,576]{3,2,1,0:T(8,128)S(1)}, u32[]{:S(2)}, u32[]{:S(2)}) collective-permute-start(f32[1,2,64,576]{3,2,1,0:T(8,128)S(1)} %broadcast_multiply_fusion), channel_id=1, source_target_pairs={{32,0},{64,32},{96,64},{128,96},{160,128},{192,160},{224,192},{256... | collective-permute-start | bytes 884744 | tf_op jit(solution)/shard_map/ppermute | solution.py:20
  11.8 24.4 %collective-permute-start.2 = (f32[3,1,64,576]{3,2,1,0:T(8,128)S(1)}, f32[3,1,64,576]{3,2,1,0:T(8,128)S(1)}, u32[]{:S(2)}, u32[]{:S(2)}) collective-permute-start(f32[3,1,64,576]{3,2,1,0:T(8,128)S(1)} %get-tuple-element.125), channel_id=1, source_target_pairs={{0,1},{1,2},{2,3},{3,4},{4,5},{5,6},{6,7},{7,8},{8,9},{9,10},{10,1... | collective-permute-start | bytes 1327112 | tf_op jit(solution)/shard_map/ppermute | solution.py:18
  15.0 22.3 %collective-permute-start.3 = (f32[3,1,64,576]{3,2,1,0:T(8,128)S(1)}, f32[3,1,64,576]{3,2,1,0:T(8,128)S(1)}, u32[]{:S(2)}, u32[]{:S(2)}) collective-permute-start(f32[3,1,64,576]{3,2,1,0:T(8,128)S(1)} %get-tuple-element.126), channel_id=1, source_target_pairs={{1,0},{2,1},{3,2},{4,3},{5,4},{6,5},{7,6},{8,7},{9,8},{10,9},{11,1... | collective-permute-start | bytes 1327112 | tf_op jit(solution)/shard_map/ppermute | solution.py:20
  49.4 1.0 copy-start
  50.4 4.6 %collective-permute-start.4 = (f32[1,2,64,576]{3,2,1,0:T(8,128)S(1)}, f32[1,2,64,576]{3,2,1,0:T(8,128)S(1)}, u32[]{:S(2)}, u32[]{:S(2)}) collective-permute-start(f32[1,2,64,576]{3,2,1,0:T(8,128)S(1)} %fusion), channel_id=1, source_target_pairs={{0,32},{32,64},{64,96},{96,128},{128,160},{160,192},{192,224},{224... | collective-permute-start | bytes 884744 | tf_op jit(solution)/shard_map/ppermute | solution.py:18
  51.1 6.8 %collective-permute-start.5 = (f32[1,2,64,576]{3,2,1,0:T(8,128)S(1)}, f32[1,2,64,576]{3,2,1,0:T(8,128)S(1)}, u32[]{:S(2)}, u32[]{:S(2)}) collective-permute-start(f32[1,2,64,576]{3,2,1,0:T(8,128)S(1)} %fusion), channel_id=1, source_target_pairs={{32,0},{64,32},{96,64},{128,96},{160,128},{192,160},{224,192},{256... | collective-permute-start | bytes 884744 | tf_op jit(solution)/shard_map/ppermute | solution.py:20
  58.0 17.8 %collective-permute-start.6 = (f32[3,1,64,576]{3,2,1,0:T(8,128)S(1)}, f32[3,1,64,576]{3,2,1,0:T(8,128)S(1)}, u32[]{:S(2)}, u32[]{:S(2)}) collective-permute-start(f32[3,1,64,576]{3,2,1,0:T(8,128)S(1)} %get-tuple-element.123), channel_id=1, source_target_pairs={{0,1},{1,2},{2,3},{3,4},{4,5},{5,6},{6,7},{7,8},{8,9},{9,10},{10,1... | collective-permute-start | bytes 1327112 | tf_op jit(solution)/shard_map/ppermute | solution.py:18
  59.9 16.8 %collective-permute-start.7 = (f32[3,1,64,576]{3,2,1,0:T(8,128)S(1)}, f32[3,1,64,576]{3,2,1,0:T(8,128)S(1)}, u32[]{:S(2)}, u32[]{:S(2)}) collective-permute-start(f32[3,1,64,576]{3,2,1,0:T(8,128)S(1)} %get-tuple-element.124), channel_id=1, source_target_pairs={{1,0},{2,1},{3,2},{4,3},{5,4},{6,5},{7,6},{8,7},{9,8},{10,9},{11,1... | collective-permute-start | bytes 1327112 | tf_op jit(solution)/shard_map/ppermute | solution.py:20
  89.7 5.6 %collective-permute-start.8 = (f32[1,2,64,576]{3,2,1,0:T(8,128)S(1)}, f32[1,2,64,576]{3,2,1,0:T(8,128)S(1)}, u32[]{:S(2)}, u32[]{:S(2)}) collective-permute-start(f32[1,2,64,576]{3,2,1,0:T(8,128)S(1)} %fusion.1), channel_id=1, source_target_pairs={{0,32},{32,64},{64,96},{96,128},{128,160},{160,192},{192,224},{224... | collective-permute-start | bytes 884744 | tf_op jit(solution)/shard_map/ppermute | solution.py:18
  91.3 6.8 %collective-permute-start.9 = (f32[1,2,64,576]{3,2,1,0:T(8,128)S(1)}, f32[1,2,64,576]{3,2,1,0:T(8,128)S(1)}, u32[]{:S(2)}, u32[]{:S(2)}) collective-permute-start(f32[1,2,64,576]{3,2,1,0:T(8,128)S(1)} %fusion.1), channel_id=1, source_target_pairs={{32,0},{64,32},{96,64},{128,96},{160,128},{192,160},{224,192},{256... | collective-permute-start | bytes 884744 | tf_op jit(solution)/shard_map/ppermute | solution.py:20
  98.2 17.5 %collective-permute-start.10 = (f32[3,1,64,576]{3,2,1,0:T(8,128)S(1)}, f32[3,1,64,576]{3,2,1,0:T(8,128)S(1)}, u32[]{:S(2)}, u32[]{:S(2)}) collective-permute-start(f32[3,1,64,576]{3,2,1,0:T(8,128)S(1)} %get-tuple-element.121), channel_id=1, source_target_pairs={{0,1},{1,2},{2,3},{3,4},{4,5},{5,6},{6,7},{7,8},{8,9},{9,10},{10,1... | collective-permute-start | bytes 1327112 | tf_op jit(solution)/shard_map/ppermute | solution.py:18
  100.2 16.5 %collective-permute-start.11 = (f32[3,1,64,576]{3,2,1,0:T(8,128)S(1)}, f32[3,1,64,576]{3,2,1,0:T(8,128)S(1)}, u32[]{:S(2)}, u32[]{:S(2)}) collective-permute-start(f32[3,1,64,576]{3,2,1,0:T(8,128)S(1)} %get-tuple-element.122), channel_id=1, source_target_pairs={{1,0},{2,1},{3,2},{4,3},{5,4},{6,5},{7,6},{8,7},{9,8},{10,9},{11,1... | collective-permute-start | bytes 1327112 | tf_op jit(solution)/shard_map/ppermute | solution.py:20
  132.9 5.6 %collective-permute-start.12 = (f32[1,2,64,576]{3,2,1,0:T(8,128)S(1)}, f32[1,2,64,576]{3,2,1,0:T(8,128)S(1)}, u32[]{:S(2)}, u32[]{:S(2)}) collective-permute-start(f32[1,2,64,576]{3,2,1,0:T(8,128)S(1)} %fusion.2), channel_id=1, source_target_pairs={{0,32},{32,64},{64,96},{96,128},{128,160},{160,192},{192,224},{224... | collective-permute-start | bytes 884744 | tf_op jit(solution)/shard_map/ppermute | solution.py:18
  134.5 6.8 %collective-permute-start.13 = (f32[1,2,64,576]{3,2,1,0:T(8,128)S(1)}, f32[1,2,64,576]{3,2,1,0:T(8,128)S(1)}, u32[]{:S(2)}, u32[]{:S(2)}) collective-permute-start(f32[1,2,64,576]{3,2,1,0:T(8,128)S(1)} %fusion.2), channel_id=1, source_target_pairs={{32,0},{64,32},{96,64},{128,96},{160,128},{192,160},{224,192},{256... | collective-permute-start | bytes 884744 | tf_op jit(solution)/shard_map/ppermute | solution.py:20
  141.4 17.3 %collective-permute-start.14 = (f32[3,1,64,576]{3,2,1,0:T(8,128)S(1)}, f32[3,1,64,576]{3,2,1,0:T(8,128)S(1)}, u32[]{:S(2)}, u32[]{:S(2)}) collective-permute-start(f32[3,1,64,576]{3,2,1,0:T(8,128)S(1)} %get-tuple-element.119), channel_id=1, source_target_pairs={{0,1},{1,2},{2,3},{3,4},{4,5},{5,6},{6,7},{7,8},{8,9},{9,10},{10,1... | collective-permute-start | bytes 1327112 | tf_op jit(solution)/shard_map/ppermute | solution.py:18
  143.3 16.2 %collective-permute-start.15 = (f32[3,1,64,576]{3,2,1,0:T(8,128)S(1)}, f32[3,1,64,576]{3,2,1,0:T(8,128)S(1)}, u32[]{:S(2)}, u32[]{:S(2)}) collective-permute-start(f32[3,1,64,576]{3,2,1,0:T(8,128)S(1)} %get-tuple-element.120), channel_id=1, source_target_pairs={{1,0},{2,1},{3,2},{4,3},{5,4},{6,5},{7,6},{8,7},{9,8},{10,9},{11,1... | collective-permute-start | bytes 1327112 | tf_op jit(solution)/shard_map/ppermute | solution.py:20
  175.8 5.8 %collective-permute-start.16 = (f32[1,2,64,576]{3,2,1,0:T(8,128)S(1)}, f32[1,2,64,576]{3,2,1,0:T(8,128)S(1)}, u32[]{:S(2)}, u32[]{:S(2)}) collective-permute-start(f32[1,2,64,576]{3,2,1,0:T(8,128)S(1)} %fusion.3), channel_id=1, source_target_pairs={{0,32},{32,64},{64,96},{96,128},{128,160},{160,192},{192,224},{224... | collective-permute-start | bytes 884744 | tf_op jit(solution)/shard_map/ppermute | solution.py:18
  177.6 6.8 %collective-permute-start.17 = (f32[1,2,64,576]{3,2,1,0:T(8,128)S(1)}, f32[1,2,64,576]{3,2,1,0:T(8,128)S(1)}, u32[]{:S(2)}, u32[]{:S(2)}) collective-permute-start(f32[1,2,64,576]{3,2,1,0:T(8,128)S(1)} %fusion.3), channel_id=1, source_target_pairs={{32,0},{64,32},{96,64},{128,96},{160,128},{192,160},{224,192},{256... | collective-permute-start | bytes 884744 | tf_op jit(solution)/shard_map/ppermute | solution.py:20
  184.6 17.2 %collective-permute-start.18 = (f32[3,1,64,576]{3,2,1,0:T(8,128)S(1)}, f32[3,1,64,576]{3,2,1,0:T(8,128)S(1)}, u32[]{:S(2)}, u32[]{:S(2)}) collective-permute-start(f32[3,1,64,576]{3,2,1,0:T(8,128)S(1)} %get-tuple-element.117), channel_id=1, source_target_pairs={{0,1},{1,2},{2,3},{3,4},{4,5},{5,6},{6,7},{7,8},{8,9},{9,10},{10,1... | collective-permute-start | bytes 1327112 | tf_op jit(solution)/shard_map/ppermute | solution.py:18
  186.5 16.2 %collective-permute-start.19 = (f32[3,1,64,576]{3,2,1,0:T(8,128)S(1)}, f32[3,1,64,576]{3,2,1,0:T(8,128)S(1)}, u32[]{:S(2)}, u32[]{:S(2)}) collective-permute-start(f32[3,1,64,576]{3,2,1,0:T(8,128)S(1)} %get-tuple-element.118), channel_id=1, source_target_pairs={{1,0},{2,1},{3,2},{4,3},{5,4},{6,5},{7,6},{8,7},{9,8},{10,9},{11,1... | collective-permute-start | bytes 1327112 | tf_op jit(solution)/shard_map/ppermute | solution.py:20
  218.9 106.0 %copy-start.1 = (f32[1,2,64,576]{3,2,1,0:T(8,128)}, f32[1,2,64,576]{3,2,1,0:T(8,128)S(1)}, u32[]{:S(2)}) copy-start(f32[1,2,64,576]{3,2,1,0:T(8,128)S(1)} %fusion.4) | copy-start | bytes 884740
where the time goes:
time: 326 us; the launch traced here: 325 us
  blocking collectives  102 us (31%)
  waiting for transfers between devices  68.8 us (21%)
  starting transfers between devices  68 us (21%)
  local copies, waits for them, and re-layouts  43.4 us (13%)
  matrix products  25.5 us (8%)
  other arithmetic  9.39 us (3%)
  between operations  8.22 us (3%)
    psum x1, blocking collectives, on_device(): occupations.append(lax.psum(local_sum, ('row', 'col')) / matrix_order)  102 us
    ppermute x10, waiting for transfers between devices, padded(): lax.ppermute(tail, axis, [(i, (i + 1) % count) for i in range(count)])  52 us
    ppermute x10, starting transfers between devices, padded(): lax.ppermute(head, axis, [((i + 1) % count, i) for i in range(count)])  49 us
    slice x10, local copies, waits for them, and re-layouts, square_blocks(): neighbour[:, :, :, reach_a + 1, (lowest + 1) * block_size:(highest + 2) *...  25.6 us
    dot_general x105, matrix products, square_blocks(): jnp.einsum('abrk,abkx->abrx', left_block, right_block, precision=lax.Prec...  25.5 us
    ppermute x10, starting transfers between devices, padded(): lax.ppermute(tail, axis, [(i, (i + 1) % count) for i in range(count)])  19.1 us
    ppermute x10, waiting for transfers between devices, padded(): lax.ppermute(head, axis, [((i + 1) % count, i) for i in range(count)])  16.8 us
    reshape x5, local copies, waits for them, and re-layouts, square_blocks(): extended.reshape(row_count + 2, col_count + 2, block_size, 3, 3 * block_s...  15.1 us
  transfers between devices with their start and end apart: 20, of which 20 were waited for; matrix products, arithmetic and copies ran while one was open for 0% of the time, Pallas kernels for 0%

commit v1 on v0

v1 whole, which is shorter than its diff:
```python
import functools

import jax
import jax.numpy as jnp
from jax import lax
from jax.experimental import pallas as pl
from jax.experimental.pallas import tpu as pltpu
from jax.sharding import PartitionSpec as P

ITERS = 5
BLK = 64
MESH = pl.DeviceIdType.MESH


def split(value):
    high = value.astype(jnp.bfloat16)
    low = (value - high.astype(jnp.float32)).astype(jnp.bfloat16)
    return high, low


def dot(a, b, transposed=False):
    dims = (((1,), (1,)), ((), ())) if transposed else (((1,), (0,)), ((), ()))
    return lax.dot_general(a, b, dims, preferred_element_type=jnp.float32)


def kernel(
    rows,
    cols,
    order,
    branch_ref,
    pattern_ref,
    initial_ref,
    density_ref,
    occupation_ref,
    x,
    hbuf,
    vbuf,
    cbuf,
    masks,
    pair,
    mid_hi,
    mid_lo,
    out_hi,
    out_lo,
    stats,
    reduced,
    h_send,
    h_recv,
    v_send,
    v_recv,
    c_send,
    c_recv,
    r_send,
    r_recv,
):
    row, col = lax.axis_index("row"), lax.axis_index("col")
    left = (row, lax.rem(col + cols - 1, cols))
    right = (row, lax.rem(col + 1, cols))
    top = (lax.rem(row + rows - 1, rows), col)
    bottom = (lax.rem(row + 1, rows), col)

    ys, zs, xs = rows // 2, max(cols // 4, 1), min(cols, 4)
    y, core = row // 2, lax.rem(row, 2)
    z, xx = col // xs, lax.rem(col, xs)

    def member(phase, index):
        if phase == 0:
            return (index * 2 + core, col)
        if phase == 1:
            return (row, index * xs + xx)
        return (y * 2 + index // xs, z * xs + lax.rem(index, xs))

    own = (y, z, core * xs + xx)
    sizes = (ys, zs, 2 * xs)

    barrier = pltpu.get_barrier_semaphore()
    for device in (left, right, top, bottom):
        pl.semaphore_signal(barrier, inc=1, device_id=device, device_id_type=MESH)
    for phase in range(3):
        for step in range(1, sizes[phase]):
            device = member(phase, lax.rem(own[phase] + step, sizes[phase]))
            pl.semaphore_signal(barrier, inc=1, device_id=device, device_id_type=MESH)

    lane = lax.broadcasted_iota(jnp.int32, (BLK, 2 * BLK), 1)
    zero = jnp.zeros((BLK, BLK), jnp.float32)

    def pattern(atom, k):
        return pattern_ref[0, atom, k].astype(jnp.float32)

    for g in range(3):
        k = 3 * g
        masks[g, 0, 0:BLK] = jnp.where(lane < BLK, pattern(0, k), pattern(0, k + 1))
        masks[g, 1, 0:BLK] = jnp.where(lane < BLK, pattern(0, k + 2), 0.0)
        masks[g, 0, BLK : 2 * BLK] = jnp.where(lane < BLK, 0.0, pattern(1, k))
        masks[g, 1, BLK : 2 * BLK] = jnp.where(lane < BLK, pattern(1, k + 1), pattern(1, k + 2))
        base = k * BLK
        first = initial_ref[0, 0, :, base : base + 3 * BLK]
        second = initial_ref[0, 1, :, base : base + 3 * BLK]
        x[0, g, 0, 0:BLK] = first[:, : 2 * BLK] * masks[g, 0, 0:BLK]
        x[0, g, 1, 0:BLK] = jnp.concatenate([first[:, 2 * BLK :], zero], axis=1) * masks[g, 1, 0:BLK]
        x[0, g, 0, BLK : 2 * BLK] = (
            jnp.concatenate([zero, second[:, :BLK]], axis=1) * masks[g, 0, BLK : 2 * BLK]
        )
        x[0, g, 1, BLK : 2 * BLK] = second[:, BLK:] * masks[g, 1, BLK : 2 * BLK]

    def send_h(i, g):
        return [
            pltpu.make_async_remote_copy(
                x.at[i, g, 1, pl.ds(BLK, BLK)],
                hbuf.at[i, 0, g],
                h_send.at[i, 0, g],
                h_recv.at[i, 0, g],
                device_id=right,
                device_id_type=MESH,
            ),
            pltpu.make_async_remote_copy(
                x.at[i, g, 0, pl.ds(0, BLK)],
                hbuf.at[i, 1, g],
                h_send.at[i, 1, g],
                h_recv.at[i, 1, g],
                device_id=left,
                device_id_type=MESH,
            ),
        ]

    def send_v(i):
        return [
            pltpu.make_async_remote_copy(
                x.at[i, 1],
                vbuf.at[i, side],
                v_send.at[i, side],
                v_recv.at[i, side],
                device_id=device,
                device_id_type=MESH,
            )
            for side, device in ((0, bottom), (1, top))
        ]

    def send_c(i):
        return [
            pltpu.make_async_remote_copy(
                hbuf.at[i, side, 1],
                cbuf.at[i, line, side],
                c_send.at[i, line, side],
                c_recv.at[i, line, side],
                device_id=device,
                device_id_type=MESH,
            )
            for line, device in ((0, bottom), (1, top))
            for side in (0, 1)
        ]

    def start(copies):
        for copy in copies:
            copy.start()

    def wait_recv(copies):
        for copy in copies:
            copy.wait_recv()

    def wait_send(copies):
        for copy in copies:
            copy.wait_send()

    wide_zero = jnp.zeros((BLK, 2 * BLK), jnp.bfloat16)
    for ref in (mid_hi, mid_lo):
        for g in range(3):
            base = g * 4 * BLK
            ref[0:BLK, base + 2 * BLK : base + 4 * BLK] = wide_zero
            ref[3 * BLK : 4 * BLK, base : base + 2 * BLK] = wide_zero
    for ref in (out_hi, out_lo):
        for line in range(2):
            ref[line, 0:BLK, 2 * BLK : 4 * BLK] = wide_zero
            ref[line, 3 * BLK : 4 * BLK, 0 : 2 * BLK] = wide_zero
    stats[...] = jnp.zeros_like(stats)

    pl.semaphore_wait(barrier, 4 + sum(size - 1 for size in sizes))

    start(send_h(0, 1))
    start(send_v(0))
    start(send_h(0, 0))
    start(send_h(0, 2))

    r_iota = lax.broadcasted_iota(jnp.int32, (2 * BLK, 2 * BLK), 0)
    l_iota = lax.broadcasted_iota(jnp.int32, (2 * BLK, 2 * BLK), 1)
    s_iota = lax.broadcasted_iota(jnp.int32, (8, 2 * BLK), 0)

    def fold(value):
        return jnp.sum(value, axis=0, keepdims=True)

    def add_stats(i):
        norm = jnp.zeros((2 * BLK, 2 * BLK), jnp.float32)
        for g in range(3):
            for half in range(2):
                norm = norm + x[i, g, half] * x[i, g, half]
        norm = fold(norm)
        trace = fold(
            jnp.where(l_iota == r_iota + BLK, x[i, 1, 0], 0.0)
            + jnp.where(l_iota + BLK == r_iota, x[i, 1, 1], 0.0)
        )
        occupied = jnp.where(branch_ref[i] == 0, norm, 2.0 * trace - norm)
        stats[...] = jnp.where(s_iota == i, occupied, stats[...])

    def own_operands(i):
        for g in range(3):
            for half in range(2):
                high, low = split(x[i, g, half])
                base = g * 4 * BLK + half * 2 * BLK
                pair[0 : 2 * BLK, base : base + 2 * BLK] = high
                pair[2 * BLK : 4 * BLK, base : base + 2 * BLK] = low
                mid_hi[BLK : 3 * BLK, base : base + 2 * BLK] = high
                mid_lo[BLK : 3 * BLK, base : base + 2 * BLK] = low

    def mid_operands(i, g):
        for side in range(2):
            high, low = split(hbuf[i, side, g])
            base = g * 4 * BLK + side * 2 * BLK
            lines = slice(side * 3 * BLK, side * 3 * BLK + BLK)
            mid_hi[lines, base : base + 2 * BLK] = high
            mid_lo[lines, base : base + 2 * BLK] = low

    def vertical_operands(i, line):
        for half in range(2):
            high, low = split(vbuf[i, line, half])
            lanes = slice(half * 2 * BLK, half * 2 * BLK + 2 * BLK)
            out_hi[line, BLK : 3 * BLK, lanes] = high
            out_lo[line, BLK : 3 * BLK, lanes] = low

    def corner_operands(i, line):
        for side in range(2):
            high, low = split(cbuf[i, line, side])
            lanes = slice(side * 2 * BLK, side * 2 * BLK + 2 * BLK)
            lines = slice(side * 3 * BLK, side * 3 * BLK + BLK)
            out_hi[line, lines, lanes] = high
            out_lo[line, lines, lanes] = low

    wide = 4 * BLK

    def square_mid():
        both = dot(pair[...], mid_hi[...], True)
        return both[: 2 * BLK] + both[2 * BLK :] + dot(pair[0 : 2 * BLK], mid_lo[...], True)

    def square_out(line):
        g = 2 * line
        lanes = slice(g * wide, g * wide + wide)
        inner = slice(wide, 2 * wide)
        both = dot(pair[:, lanes], out_hi[line]) + dot(pair[:, inner], mid_hi[:, lanes])
        cross = dot(pair[0 : 2 * BLK, lanes], out_lo[line]) + dot(pair[0 : 2 * BLK, inner], mid_lo[:, lanes])
        return both[: 2 * BLK] + both[2 * BLK :] + cross

    def update(i, g, square):
        results = []
        for half in range(2):
            part = square[:, half * 2 * BLK : half * 2 * BLK + 2 * BLK]
            new = jnp.where(branch_ref[i] == 0, part, 2.0 * x[i, g, half] - part)
            results.append(new * masks[g, half])
        return results

    def store_x(i, g, results):
        for half in range(2):
            x[i + 1, g, half] = results[half]

    def store_out(g, results):
        base = 3 * g * BLK
        density_ref[0, 0, :, base : base + 3 * BLK] = jnp.concatenate(
            [results[0][:BLK], results[1][:BLK, :BLK]], axis=1
        )
        density_ref[0, 1, :, base : base + 3 * BLK] = jnp.concatenate(
            [results[0][BLK:, BLK:], results[1][BLK:]], axis=1
        )

    def reduce_copies(phase):
        return [
            pltpu.make_async_remote_copy(
                reduced.at[phase, own[phase]],
                reduced.at[phase, own[phase]],
                r_send.at[phase, step],
                r_recv.at[phase, step],
                device_id=member(phase, lax.rem(own[phase] + step, sizes[phase])),
                device_id_type=MESH,
            )
            for step in range(1, sizes[phase])
        ]

    def reduce_begin(phase, value):
        reduced[phase, own[phase]] = value
        copies = reduce_copies(phase)
        start(copies)
        return copies

    def reduce_end(phase, copies):
        wait_recv(copies)
        total = reduced[phase, 0]
        for index in range(1, sizes[phase]):
            total = total + reduced[phase, index]
        return total

    def body(i, carry):
        wait_recv(send_h(i, 1))
        start(send_c(i))
        add_stats(i)
        own_operands(i)
        wait_recv(send_h(i, 0))
        wait_recv(send_h(i, 2))
        for g in range(3):
            mid_operands(i, g)
        store_x(i, 1, update(i, 1, square_mid()))
        start(send_h(i + 1, 1))
        start(send_v(i + 1))
        wait_recv(send_v(i))
        wait_recv(send_c(i))
        for line in range(2):
            vertical_operands(i, line)
            corner_operands(i, line)
            store_x(i, 2 * line, update(i, 2 * line, square_out(line)))
            start(send_h(i + 1, 2 * line))
        return carry

    lax.fori_loop(0, ITERS - 1, body, 0)

    last = ITERS - 1
    wait_recv(send_h(last, 1))
    start(send_c(last))
    add_stats(last)
    copies0 = reduce_begin(0, stats[...])
    own_operands(last)
    wait_recv(send_h(last, 0))
    wait_recv(send_h(last, 2))
    for g in range(3):
        mid_operands(last, g)
    store_out(1, update(last, 1, square_mid()))
    copies1 = reduce_begin(1, reduce_end(0, copies0))
    wait_recv(send_v(last))
    wait_recv(send_c(last))
    vertical_operands(last, 0)
    corner_operands(last, 0)
    store_out(0, update(last, 0, square_out(0)))
    copies2 = reduce_begin(2, reduce_end(1, copies1))
    vertical_operands(last, 1)
    corner_operands(last, 1)
    store_out(2, update(last, 2, square_out(1)))
    total = reduce_end(2, copies2)
    for i in range(ITERS):
        occupation_ref[i] = jnp.sum(total[i : i + 1]) / order

    def drain(i, carry):
        for g in range(3):
            wait_send(send_h(i, g))
        wait_send(send_v(i))
        wait_send(send_c(i))
        return carry

    lax.fori_loop(0, ITERS, drain, 0)
    wait_send(copies0)
    wait_send(copies1)
    wait_send(copies2)


def on_device(rows, cols, order, initial, pattern, branch):
    half = 2 * BLK
    wide = 4 * BLK
    sizes = (rows // 2, max(cols // 4, 1), 2 * min(cols, 4))
    slots = max(sizes)
    vmem = pl.BlockSpec(memory_space=pltpu.VMEM)
    smem = pl.BlockSpec(memory_space=pltpu.SMEM)
    dma = pltpu.SemaphoreType.DMA
    return pl.pallas_call(
        functools.partial(kernel, rows, cols, order),
        out_shape=(
            jax.ShapeDtypeStruct(initial.shape, jnp.float32),
            jax.ShapeDtypeStruct((ITERS,), jnp.float32),
        ),
        in_specs=[smem, smem, vmem],
        out_specs=(vmem, smem),
        scratch_shapes=[
            pltpu.VMEM((ITERS, 3, 2, half, half), jnp.float32),
            pltpu.VMEM((ITERS, 2, 3, BLK, half), jnp.float32),
            pltpu.VMEM((ITERS, 2, 2, half, half), jnp.float32),
            pltpu.VMEM((ITERS, 2, 2, BLK, half), jnp.float32),
            pltpu.VMEM((3, 2, half, half), jnp.float32),
            pltpu.VMEM((wide, 3 * wide), jnp.bfloat16),
            pltpu.VMEM((wide, 3 * wide), jnp.bfloat16),
            pltpu.VMEM((wide, 3 * wide), jnp.bfloat16),
            pltpu.VMEM((2, wide, wide), jnp.bfloat16),
            pltpu.VMEM((2, wide, wide), jnp.bfloat16),
            pltpu.VMEM((8, half), jnp.float32),
            pltpu.VMEM((3, slots, 8, half), jnp.float32),
            dma((ITERS, 2, 3)),
            dma((ITERS, 2, 3)),
            dma((ITERS, 2)),
            dma((ITERS, 2)),
            dma((ITERS, 2, 2)),
            dma((ITERS, 2, 2)),
            dma((3, slots)),
            dma((3, slots)),
        ],
        compiler_params=pltpu.CompilerParams(
            collective_id=0, has_side_effects=True, vmem_limit_bytes=32 * 1024 * 1024
        ),
        cost_estimate=pl.CostEstimate(flops=1800000000, bytes_accessed=600000, transcendentals=0),
    )(branch, pattern, initial)


def solution(mesh):
    rows, cols = mesh.shape["row"], mesh.shape["col"]

    def program(initial, pattern, branch):
        order = initial.shape[0] * initial.shape[1] * initial.shape[2]
        return jax.shard_map(
            functools.partial(on_device, rows, cols, float(order)),
            mesh=mesh,
            in_specs=(P("row", "col", None, None), P("row", "col", None), P()),
            out_specs=(P("row", "col", None, None), P()),
            check_vma=False,
        )(initial, pattern, branch)

    return program
```

time: 326 us -> 65.2 us (0.20)
  blocking collectives: 102 us -> 0 us
  waiting for transfers between devices: 68.8 us -> 0 us
  starting transfers between devices: 68 us -> 0 us
  Pallas kernels: 0 us -> 60.6 us
  local copies, waits for them, and re-layouts: 43.4 us -> 3.54 us
  matrix products: 25.5 us -> 0 us
  other arithmetic: 9.39 us -> 0 us
  between operations: 8.22 us -> 0.65 us
    psum x1 -> x0, blocking collectives: 102 us -> none  [on_device(): occupations.append(lax.psum(local_sum, ('row', 'col')) / matrix_order)]
    ppermute x20 -> x0, waiting for transfers between devices: 68.8 us -> none  [the longest x10 52 us: padded(): lax.ppermute(tail, axis, [(i, (i + 1) % count) for i in range(count)])]
    ppermute x20 -> x0, starting transfers between devices: 68 us -> none  [the longest x10 49 us: padded(): lax.ppermute(head, axis, [((i + 1) % count, i) for i in range(count)])]
    pallas_call x0 -> x1, Pallas kernels: none -> 60.6 us  [on_device(): pl.pallas_call(functools.partial(kernel, rows, cols, order), out_shape=(j...]
    slice x16 -> x0, local copies, waits for them, and re-layouts: 26.6 us -> none  [the longest x10 25.6 us: square_blocks(): neighbour[:, :, :, reach_a + 1, (lowest + 1) * block_size:(highest + 2) *...]
    dot_general x105 -> x0, matrix products: 25.5 us -> none  [square_blocks(): jnp.einsum('abrk,abkx->abrx', left_block, right_block, precision=lax.Prec...]
    reshape x5 -> x0, local copies, waits for them, and re-layouts: 15.1 us -> none  [square_blocks(): extended.reshape(row_count + 2, col_count + 2, block_size, 3, 3 * block_s...]
    concatenate x10 -> x0, other arithmetic: 3.78 us -> none  [padded(): jnp.concatenate([lax.ppermute(tail, axis, [(i, (i + 1) % count) for i in...]
  transfers between devices with their start and end apart: 20 -> 0, of which waited for: 20 -> 0; matrix products, arithmetic and copies ran while one was open for 0% -> 0% of each run, Pallas kernels for 0% -> 0%
where the time goes in v1:
time: 65.2 us; the launch traced here: 64.8 us
  Pallas kernels  60.6 us (93%)
  local copies, waits for them, and re-layouts  3.54 us (5%)
    pallas_call x1, Pallas kernels, on_device(): pl.pallas_call(functools.partial(kernel, rows, cols, order), out_shape=(j...  60.6 us
    unnamed x8, local copies, waits for them, and re-layouts  3.54 us

profile of v1, /device:TPU:1, one launch (start us, length us, event | category | flops | bytes accessed | tf_op | source)
XLA Modules:
  0.0 64.8 jit_solution(14013931460110759981)
XLA Ops:
  0.6 0.0 copy-start
  0.6 1.0 %copy-done = f32[1,2,64,576]{3,2,1,0:T(8,128)S(1)} copy-done((f32[1,2,64,576]{3,2,1,0:T(8,128)S(1)}, f32[1,2,64,576]{3,2,1,0:T(8,128)}, u32[]{:S(2)}) %copy-start) | copy-done | bytes 294936
  1.6 0.0 copy-start.1
  1.6 0.7 %copy-done.1 = s32[1,2,9]{2,1,0:T(2,128)S(1)} copy-done((s32[1,2,9]{2,1,0:T(2,128)S(1)}, s32[1,2,9]{2,1,0:T(2,128)}, u32[]{:S(2)}) %copy-start.1) | copy-done | bytes 96
  2.3 0.0 copy-start.2
  2.3 0.7 %copy-done.2 = s32[5]{0:T(128)S(1)} copy-done((s32[5]{0:T(128)S(1)}, s32[5]{0:T(128)}, u32[]{:S(2)}) %copy-start.2) | copy-done | bytes 44
  2.9 60.6 %shard_map.50 = (f32[1,2,64,576]{3,2,1,0:T(8,128)S(1)}, f32[5]{0:T(128)S(1)}) custom-call(s32[5]{0:T(128)S(1)} %copy-done.2, s32[1,2,9]{2,1,0:T(2,128)S(1)} %copy-done.1, f32[1,2,64,576]{3,2,1,0:T(8,128)S(1)} %copy-done), custom_call_target="tpu_custom_call" | custom-call | flops 1800000000 | bytes 600000 | tf_op jit(solution)/shard_map/pallas_call | solution.py:367
  63.6 0.7 %copy.7 = f32[1,2,64,576]{3,2,1,0:T(8,128)} copy(f32[1,2,64,576]{3,2,1,0:T(8,128)S(1)} %get-tuple-element.4) | data formatting | bytes 589824
  64.3 0.5 copy.8
Async XLA Ops:
  0.6 1.0 %copy-start = (f32[1,2,64,576]{3,2,1,0:T(8,128)S(1)}, f32[1,2,64,576]{3,2,1,0:T(8,128)}, u32[]{:S(2)}) copy-start(f32[1,2,64,576]{3,2,1,0:T(8,128)} %initial_ref.1) | copy-start | bytes 884740
  1.6 0.7 %copy-start.1 = (s32[1,2,9]{2,1,0:T(2,128)S(1)}, s32[1,2,9]{2,1,0:T(2,128)}, u32[]{:S(2)}) copy-start(s32[1,2,9]{2,1,0:T(2,128)} %pattern_ref.1) | copy-start | bytes 220
  2.3 0.7 %copy-start.2 = (s32[5]{0:T(128)S(1)}, s32[5]{0:T(128)}, u32[]{:S(2)}) copy-start(s32[5]{0:T(128)} %branch_ref.1) | copy-start | bytes 64

commit v2 on v1

v2 whole, which is shorter than its diff:
```python
import functools

import jax
import jax.numpy as jnp
from jax import lax
from jax.experimental import pallas as pl
from jax.experimental.pallas import tpu as pltpu
from jax.sharding import PartitionSpec as P

ITERS = 5
BLK = 64
MESH = pl.DeviceIdType.MESH


def split(value):
    high = value.astype(jnp.bfloat16)
    low = (value - high.astype(jnp.float32)).astype(jnp.bfloat16)
    return high, low


def dot(a, b, transposed=False):
    dims = (((1,), (1,)), ((), ())) if transposed else (((1,), (0,)), ((), ()))
    return lax.dot_general(a, b, dims, preferred_element_type=jnp.float32)


def beside(a, b):
    return jnp.concatenate([a, b], axis=1)


def pack(block):
    return beside(block[: BLK // 2], block[BLK // 2 :])


def unpack(packed):
    return jnp.concatenate([packed[:, :BLK], packed[:, BLK:]], axis=0)


def kernel(
    rows,
    cols,
    order,
    branch_hbm,
    pattern_hbm,
    initial_hbm,
    density_ref,
    occupation_ref,
    branch_ref,
    pattern_ref,
    initial_ref,
    x,
    u,
    m,
    selves,
    hbuf,
    ubuf,
    mbuf,
    sbuf,
    cbuf,
    mask_x,
    mask_u,
    mask_m,
    pair,
    far_hi,
    far_lo,
    near,
    left_side,
    h_pair,
    stats,
    reduced,
    in_sem,
    h_send,
    h_recv,
    u_send,
    u_recv,
    m_send,
    m_recv,
    s_send,
    s_recv,
    c_send,
    c_recv,
    r_send,
    r_recv,
):
    row, col = lax.axis_index("row"), lax.axis_index("col")
    west, east = lax.rem(col + cols - 1, cols), lax.rem(col + 1, cols)
    north, south = lax.rem(row + rows - 1, rows), lax.rem(row + 1, rows)
    two = 2 * BLK

    ys, zs, xs = rows // 2, max(cols // 4, 1), min(cols, 4)
    y, core = row // 2, lax.rem(row, 2)
    z, xx = col // xs, lax.rem(col, xs)

    def member(phase, index):
        if phase == 0:
            return (index * 2 + core, col)
        if phase == 1:
            return (row, index * xs + xx)
        return (y * 2 + index // xs, z * xs + lax.rem(index, xs))

    own = (y, z, core * xs + xx)
    sizes = (ys, zs, 2 * xs)

    barrier = pltpu.get_barrier_semaphore()
    near_devices = [(row, west), (row, east)] + [
        (a, b) for a in (north, south) for b in (col, west, east)
    ]
    for device in near_devices:
        pl.semaphore_signal(barrier, inc=1, device_id=device, device_id_type=MESH)
    inputs = [
        pltpu.make_async_copy(initial_hbm, initial_ref, in_sem.at[0]),
        pltpu.make_async_copy(pattern_hbm, pattern_ref, in_sem.at[1]),
        pltpu.make_async_copy(branch_hbm, branch_ref, in_sem.at[2]),
    ]
    for copy in inputs:
        copy.start()
    for phase in range(3):
        for step in range(1, sizes[phase]):
            device = member(phase, lax.rem(own[phase] + step, sizes[phase]))
            pl.semaphore_signal(barrier, inc=1, device_id=device, device_id_type=MESH)

    far_hi[...] = jnp.zeros_like(far_hi)
    far_lo[...] = jnp.zeros_like(far_lo)
    near[...] = jnp.zeros_like(near)
    left_side[...] = jnp.zeros_like(left_side)
    stats[...] = jnp.zeros_like(stats)
    for copy in inputs:
        copy.wait()

    lane = lax.broadcasted_iota(jnp.int32, (BLK, two), 1)
    low_lanes = lane < BLK
    zero = jnp.zeros((BLK, BLK), jnp.float32)

    def pattern(atom, k):
        return pattern_ref[0, atom, k].astype(jnp.float32)

    for line in range(2):
        k = 6 * line
        mask_x[line, 0, 0:BLK] = jnp.where(low_lanes, pattern(0, k), pattern(0, k + 1))
        mask_x[line, 1, 0:BLK] = jnp.where(low_lanes, pattern(0, k + 2), 0.0)
        mask_x[line, 0, BLK:two] = jnp.where(low_lanes, 0.0, pattern(1, k))
        mask_x[line, 1, BLK:two] = jnp.where(low_lanes, pattern(1, k + 1), pattern(1, k + 2))
        first = initial_ref[0, 0, :, k * BLK : k * BLK + 3 * BLK]
        second = initial_ref[0, 1, :, k * BLK : k * BLK + 3 * BLK]
        x[0, line, 0, 0:BLK] = first[:, :two] * mask_x[line, 0, 0:BLK]
        x[0, line, 1, 0:BLK] = beside(first[:, two:], zero) * mask_x[line, 1, 0:BLK]
        x[0, line, 0, BLK:two] = beside(zero, second[:, :BLK]) * mask_x[line, 0, BLK:two]
        x[0, line, 1, BLK:two] = second[:, BLK:] * mask_x[line, 1, BLK:two]
    mask_u[0:BLK] = jnp.where(low_lanes, pattern(0, 4), pattern(0, 5))
    mask_u[BLK:two] = jnp.where(low_lanes, pattern(1, 3), pattern(1, 4))
    mask_m[...] = jnp.where(low_lanes, pattern(0, 3), pattern(1, 5))
    first = initial_ref[0, 0, :, 3 * BLK : 6 * BLK]
    second = initial_ref[0, 1, :, 3 * BLK : 6 * BLK]
    u[0, 0:BLK] = first[:, BLK:] * mask_u[0:BLK]
    u[0, BLK:two] = second[:, :two] * mask_u[BLK:two]
    m[0] = beside(first[:, :BLK], second[:, two:]) * mask_m[...]

    def remote(source, target, send, recv, device):
        return pltpu.make_async_remote_copy(
            source, target, send, recv, device_id=device, device_id_type=MESH
        )

    def send_h(i):
        return [
            remote(
                x.at[i, :, 1 - side, pl.ds(BLK - side * BLK, BLK)],
                hbuf.at[i, side],
                h_send.at[i, side],
                h_recv.at[i, side],
                (row, east if side == 0 else west),
            )
            for side in range(2)
        ]

    def send_u(i):
        return [
            remote(
                u.at[i],
                ubuf.at[i, line],
                u_send.at[i, line],
                u_recv.at[i, line],
                (south if line == 0 else north, col),
            )
            for line in range(2)
        ]

    def send_m(i):
        return [
            remote(
                m.at[i],
                mbuf.at[i, line],
                m_send.at[i, line],
                m_recv.at[i, line],
                (south if line == 0 else north, col),
            )
            for line in range(2)
        ]

    def send_s(i):
        return [
            remote(
                selves.at[i, 1 - side],
                sbuf.at[i, side],
                s_send.at[i, side],
                s_recv.at[i, side],
                (row, east if side == 0 else west),
            )
            for side in range(2)
        ]

    def send_c(i):
        return [
            remote(
                selves.at[i, 1 - side],
                cbuf.at[i, line, side],
                c_send.at[i, line, side],
                c_recv.at[i, line, side],
                (south if line == 0 else north, east if side == 0 else west),
            )
            for line in range(2)
            for side in range(2)
        ]

    def start(copies):
        for copy in copies:
            copy.start()

    def wait_recv(copies):
        for copy in copies:
            copy.wait_recv()

    def wait_send(copies):
        for copy in copies:
            copy.wait_send()

    def pack_selves(i, value):
        selves[i, 0] = pack(value[:BLK, :BLK])
        selves[i, 1] = pack(value[BLK:, BLK:])

    def start_own(i):
        start(send_c(i))
        start(send_u(i))
        start(send_s(i))

    pack_selves(0, u[0])
    pl.semaphore_wait(barrier, len(near_devices) + sum(size - 1 for size in sizes))
    start(send_h(0))
    start(send_m(0))
    start_own(0)

    r_iota = lax.broadcasted_iota(jnp.int32, (two, two), 0)
    l_iota = lax.broadcasted_iota(jnp.int32, (two, two), 1)
    s_iota = lax.broadcasted_iota(jnp.int32, (8, two), 0)

    def fold(value):
        return jnp.sum(value, axis=0, keepdims=True)

    def add_stats(i):
        norm = u[i] * u[i]
        for line in range(2):
            for half in range(2):
                norm = norm + x[i, line, half] * x[i, line, half]
        norm = fold(norm) + fold(m[i] * m[i])
        trace = fold(jnp.where(l_iota == r_iota, u[i], 0.0))
        occupied = jnp.where(branch_ref[i] == 0, norm, 2.0 * trace - norm)
        stats[...] = jnp.where(s_iota == i, occupied, stats[...])

    u_lanes = slice(2 * two, 3 * two)
    m_lanes = slice(3 * two, 4 * two)

    def x_lanes(line, half=None):
        base = 4 * two * line
        if half is None:
            return slice(base, base + 2 * two)
        return slice(base + half * two, base + half * two + two)

    def set_pair(lines, lanes, value):
        high, low = split(value)
        pair[lines, lanes] = high
        pair[slice(lines.start + two, lines.stop + two), lanes] = low

    def own_operands(i):
        for line in range(2):
            for half in range(2):
                set_pair(slice(0, two), x_lanes(line, half), x[i, line, half])
        set_pair(slice(0, two), u_lanes, u[i])
        edges = m[i]
        set_pair(slice(0, BLK), m_lanes, jnp.where(low_lanes, edges, 0.0))
        set_pair(slice(BLK, two), m_lanes, jnp.where(low_lanes, 0.0, edges))

    def polynomial(i, old, square, mask):
        return jnp.where(branch_ref[i] == 0, square, 2.0 * old - square) * mask

    def next_u(i):
        both = dot(pair[...], pair[...], True)
        square = both[:two, :two] + both[:two, two:] + both[two:, :two]
        return polynomial(i, u[i], square, mask_u[...])

    def own_part(line):
        high = pair[0:two, u_lanes]
        own = dot(beside(high, high), pair[:, x_lanes(line)])
        return own + dot(pair[two : 2 * two, u_lanes], pair[0:two, x_lanes(line)])

    def near_part(i):
        near[0:two, 0:two] = pair[0:two, m_lanes]
        near[0:two, two : 2 * two] = pair[two : 2 * two, m_lanes]
        ml = beside(unpack(sbuf[i, 0]), zero)
        mr = beside(zero, unpack(sbuf[i, 1]))
        for value, lines in ((ml, slice(two, two + BLK)), (mr, slice(two + BLK, 2 * two))):
            high, low = split(value)
            near[lines, 0:two] = high
            near[lines, two : 2 * two] = low
        both = dot(pair[:, u_lanes.start : m_lanes.stop], near[...])
        return both[:two, :two] + both[:two, two:] + both[two:, :two]

    def far_operands(i, line):
        above = ubuf[i, line]
        edges = mbuf[i, line]
        turned = edges.T
        pieces = (
            (0, 0, beside(unpack(cbuf[i, line, 0]), turned[:BLK])),
            (1, 0, beside(edges[:, :BLK], above[:BLK, :BLK])),
            (1, 1, beside(above[:BLK, BLK:], zero)),
            (2, 0, beside(zero, above[BLK:, :BLK])),
            (2, 1, beside(above[BLK:, BLK:], edges[:, BLK:])),
            (3, 1, beside(turned[BLK:], unpack(cbuf[i, line, 1]))),
        )
        for at, half, value in pieces:
            high, low = split(value)
            far_hi[line, at * BLK : at * BLK + BLK, half * two : half * two + two] = high
            far_lo[line, at * BLK : at * BLK + BLK, half * two : half * two + two] = low

    def far_part(line):
        both = dot(pair[:, x_lanes(line)], far_hi[line])
        return both[:two] + both[two:] + dot(pair[0:two, x_lanes(line)], far_lo[line])

    def side_operands():
        for side in range(2):
            lines = slice(side * BLK, side * BLK + BLK)
            high = pair[lines, m_lanes][:, side * BLK : side * BLK + BLK]
            low = pair[slice(two + side * BLK, two + side * BLK + BLK), m_lanes][
                :, side * BLK : side * BLK + BLK
            ]
            left_side[side, 0:BLK] = beside(high, high)
            left_side[side, BLK:two] = beside(low, jnp.zeros_like(low))

    def message_operands(i):
        for side in range(2):
            for line in range(2):
                high, low = split(hbuf[i, side, line])
                h_pair[side, 0:BLK, line * two : line * two + two] = high
                h_pair[side, BLK:two, line * two : line * two + two] = low

    def message_products():
        outer, edge = [], []
        for side in range(2):
            both = dot(left_side[side], h_pair[side])
            outer.append(both[:BLK] + both[BLK:])
            high = slice(side * BLK, side * BLK + BLK)
            low = slice(two + side * BLK, two + side * BLK + BLK)
            links = jnp.concatenate(
                [
                    beside(pair[high, x_lanes(0, side)], pair[high, x_lanes(1, side)]),
                    beside(pair[low, x_lanes(0, side)], pair[low, x_lanes(1, side)]),
                ],
                axis=0,
            )
            both = dot(links, h_pair[side], True)
            edge.append(both[:BLK, :BLK] + both[:BLK, BLK:] + both[BLK:, :BLK])
        return outer, beside(edge[0], edge[1])

    def finish(i, sums, near_sum, emit_x, emit_m):
        outer, edge = message_products()
        for line in range(2):
            for half in range(2):
                square = sums[line][:, half * two : half * two + two]
                extra = outer[half][:, line * two : line * two + two]
                top, low = square[:BLK], square[BLK:]
                if half == 0:
                    top = top + extra
                else:
                    low = low + extra
                square = jnp.concatenate([top, low], axis=0)
                emit_x(line, half, polynomial(i, x[i, line, half], square, mask_x[line, half]))
        square = jnp.where(low_lanes, near_sum[:BLK], near_sum[BLK:]) + edge
        emit_m(polynomial(i, m[i], square, mask_m[...]))

    def reduce_copies(phase):
        steps = sorted(range(1, sizes[phase]), key=lambda step: -min(step, sizes[phase] - step))
        return [
            remote(
                reduced.at[phase, own[phase]],
                reduced.at[phase, own[phase]],
                r_send.at[phase, step],
                r_recv.at[phase, step],
                member(phase, lax.rem(own[phase] + step, sizes[phase])),
            )
            for step in steps
        ]

    def reduce_begin(phase, value):
        reduced[phase, own[phase]] = value
        copies = reduce_copies(phase)
        start(copies)
        return copies

    def reduce_end(phase, copies):
        wait_recv(copies)
        total = reduced[phase, 0]
        for index in range(1, sizes[phase]):
            total = total + reduced[phase, index]
        return total

    def before_message(i):
        sums = [own_part(line) for line in range(2)]
        side_operands()
        wait_recv(send_s(i))
        near_sum = near_part(i)
        wait_recv(send_u(i))
        wait_recv(send_c(i))
        wait_recv(send_m(i))
        for line in range(2):
            far_operands(i, line)
        sums = [sums[line] + far_part(line) for line in range(2)]
        return sums, near_sum

    def body(i, carry):
        own_operands(i)
        fresh = next_u(i)
        u[i + 1] = fresh
        pack_selves(i + 1, fresh)
        start_own(i + 1)
        add_stats(i)
        sums, near_sum = before_message(i)
        wait_recv(send_h(i))
        message_operands(i)

        def emit_x(line, half, value):
            x[i + 1, line, half] = value

        def emit_m(value):
            m[i + 1] = value

        finish(i, sums, near_sum, emit_x, emit_m)
        start(send_h(i + 1))
        start(send_m(i + 1))
        return carry

    lax.fori_loop(0, ITERS - 1, body, 0)

    last = ITERS - 1
    add_stats(last)
    copies0 = reduce_begin(0, stats[...])
    own_operands(last)
    fresh = next_u(last)
    sums, near_sum = before_message(last)
    copies1 = reduce_begin(1, reduce_end(0, copies0))
    wait_recv(send_h(last))
    message_operands(last)
    parts = {}

    def keep_x(line, half, value):
        parts[line, half] = value

    def keep_m(value):
        parts["m"] = value

    finish(last, sums, near_sum, keep_x, keep_m)
    for line in range(2):
        base = 6 * line * BLK
        a, b = parts[line, 0], parts[line, 1]
        density_ref[0, 0, :, base : base + 3 * BLK] = beside(a[:BLK], b[:BLK, :BLK])
        density_ref[0, 1, :, base : base + 3 * BLK] = beside(a[BLK:, BLK:], b[BLK:])
    edges = parts["m"]
    density_ref[0, 0, :, 3 * BLK : 6 * BLK] = beside(edges[:, :BLK], fresh[:BLK])
    density_ref[0, 1, :, 3 * BLK : 6 * BLK] = beside(fresh[BLK:], edges[:, BLK:])
    copies2 = reduce_begin(2, reduce_end(1, copies1))

    def drain(i, carry):
        for copies in (send_h(i), send_m(i), send_u(i), send_s(i), send_c(i)):
            wait_send(copies)
        return carry

    lax.fori_loop(0, ITERS, drain, 0)
    wait_send(copies0)
    wait_send(copies1)
    total = reduce_end(2, copies2)
    for i in range(ITERS):
        occupation_ref[i] = jnp.sum(total[i : i + 1]) / order
    wait_send(copies2)


def on_device(rows, cols, order, initial, pattern, branch):
    two = 2 * BLK
    sizes = (rows // 2, max(cols // 4, 1), 2 * min(cols, 4))
    slots = max(sizes)
    vmem = pl.BlockSpec(memory_space=pltpu.VMEM)
    smem = pl.BlockSpec(memory_space=pltpu.SMEM)
    hbm = pl.BlockSpec(memory_space=pltpu.HBM)
    dma = pltpu.SemaphoreType.DMA
    f32, bf16 = jnp.float32, jnp.bfloat16
    return pl.pallas_call(
        functools.partial(kernel, rows, cols, order),
        out_shape=(
            jax.ShapeDtypeStruct(initial.shape, jnp.float32),
            jax.ShapeDtypeStruct((ITERS,), jnp.float32),
        ),
        in_specs=[hbm, hbm, hbm],
        out_specs=(vmem, smem),
        scratch_shapes=[
            pltpu.SMEM(branch.shape, jnp.int32),
            pltpu.SMEM(pattern.shape, jnp.int32),
            pltpu.VMEM(initial.shape, f32),
            pltpu.VMEM((ITERS, 2, 2, two, two), f32),
            pltpu.VMEM((ITERS, two, two), f32),
            pltpu.VMEM((ITERS, BLK, two), f32),
            pltpu.VMEM((ITERS, 2, BLK // 2, two), f32),
            pltpu.VMEM((ITERS, 2, 2, BLK, two), f32),
            pltpu.VMEM((ITERS, 2, two, two), f32),
            pltpu.VMEM((ITERS, 2, BLK, two), f32),
            pltpu.VMEM((ITERS, 2, BLK // 2, two), f32),
            pltpu.VMEM((ITERS, 2, 2, BLK // 2, two), f32),
            pltpu.VMEM((2, 2, two, two), f32),
            pltpu.VMEM((two, two), f32),
            pltpu.VMEM((BLK, two), f32),
            pltpu.VMEM((2 * two, 6 * two), bf16),
            pltpu.VMEM((2, 2 * two, 2 * two), bf16),
            pltpu.VMEM((2, 2 * two, 2 * two), bf16),
            pltpu.VMEM((2 * two, 2 * two), bf16),
            pltpu.VMEM((2, two, two), bf16),
            pltpu.VMEM((2, two, 2 * two), bf16),
            pltpu.VMEM((8, two), f32),
            pltpu.VMEM((3, slots, 8, two), f32),
            dma((3,)),
            dma((ITERS, 2)),
            dma((ITERS, 2)),
            dma((ITERS, 2)),
            dma((ITERS, 2)),
            dma((ITERS, 2)),
            dma((ITERS, 2)),
            dma((ITERS, 2)),
            dma((ITERS, 2)),
            dma((ITERS, 2, 2)),
            dma((ITERS, 2, 2)),
            dma((3, slots)),
            dma((3, slots)),
        ],
        compiler_params=pltpu.CompilerParams(
            collective_id=0, has_side_effects=True, vmem_limit_bytes=32 * 1024 * 1024
        ),
        cost_estimate=pl.CostEstimate(flops=1800000000, bytes_accessed=600000, transcendentals=0),
    )(branch, pattern, initial)


def solution(mesh):
    rows, cols = mesh.shape["row"], mesh.shape["col"]

    def program(initial, pattern, branch):
        order = initial.shape[0] * initial.shape[1] * initial.shape[2]
        return jax.shard_map(
            functools.partial(on_device, rows, cols, float(order)),
            mesh=mesh,
            in_specs=(P("row", "col", None, None), P("row", "col", None), P()),
            out_specs=(P("row", "col", None, None), P()),
            check_vma=False,
        )(initial, pattern, branch)

    return program
```

time: 65.2 us -> 58.4 us (0.90)
  Pallas kernels: 60.6 us -> 54 us
    pallas_call x1, Pallas kernels: 60.6 us -> 54 us  [on_device(): pl.pallas_call(functools.partial(kernel, rows, cols, order), out_shape=(j...]
where the time goes in v2:
time: 58.4 us; the launch traced here: 58.2 us
  Pallas kernels  54 us (92%)
  local copies, waits for them, and re-layouts  3.54 us (6%)
  between operations  0.65 us (1%)
    pallas_call x1, Pallas kernels, on_device(): pl.pallas_call(functools.partial(kernel, rows, cols, order), out_shape=(j...  54 us
    unnamed x8, local copies, waits for them, and re-layouts  3.54 us

profile of v2, /device:TPU:1, one launch (start us, length us, event | category | flops | bytes accessed | tf_op | source)
XLA Modules:
  0.0 58.2 jit_solution(13450992920821683334)
XLA Ops:
  0.6 0.0 copy-start
  0.6 1.0 %copy-done = f32[1,2,64,576]{3,2,1,0:T(8,128)S(1)} copy-done((f32[1,2,64,576]{3,2,1,0:T(8,128)S(1)}, f32[1,2,64,576]{3,2,1,0:T(8,128)}, u32[]{:S(2)}) %copy-start) | copy-done | bytes 294936
  1.6 0.0 copy-start.1
  1.6 0.7 %copy-done.1 = s32[1,2,9]{2,1,0:T(2,128)S(1)} copy-done((s32[1,2,9]{2,1,0:T(2,128)S(1)}, s32[1,2,9]{2,1,0:T(2,128)}, u32[]{:S(2)}) %copy-start.1) | copy-done | bytes 96
  2.3 0.0 copy-start.2
  2.3 0.7 %copy-done.2 = s32[5]{0:T(128)S(1)} copy-done((s32[5]{0:T(128)S(1)}, s32[5]{0:T(128)}, u32[]{:S(2)}) %copy-start.2) | copy-done | bytes 44
  2.9 54.0 %shard_map.50 = (f32[1,2,64,576]{3,2,1,0:T(8,128)S(1)}, f32[5]{0:T(128)S(1)}) custom-call(s32[5]{0:T(128)S(1)} %copy-done.2, s32[1,2,9]{2,1,0:T(2,128)S(1)} %copy-done.1, f32[1,2,64,576]{3,2,1,0:T(8,128)S(1)} %copy-done), custom_call_target="tpu_custom_call" | custom-call | flops 1800000000 | bytes 600000 | tf_op jit(solution)/shard_map/pallas_call | solution.py:501
  56.9 0.7 %copy.7 = f32[1,2,64,576]{3,2,1,0:T(8,128)} copy(f32[1,2,64,576]{3,2,1,0:T(8,128)S(1)} %get-tuple-element.4) | data formatting | bytes 589824
  57.7 0.5 copy.8
Async XLA Ops:
  0.6 1.0 %copy-start = (f32[1,2,64,576]{3,2,1,0:T(8,128)S(1)}, f32[1,2,64,576]{3,2,1,0:T(8,128)}, u32[]{:S(2)}) copy-start(f32[1,2,64,576]{3,2,1,0:T(8,128)} %initial_hbm.1) | copy-start | bytes 884740
  1.6 0.7 %copy-start.1 = (s32[1,2,9]{2,1,0:T(2,128)S(1)}, s32[1,2,9]{2,1,0:T(2,128)}, u32[]{:S(2)}) copy-start(s32[1,2,9]{2,1,0:T(2,128)} %pattern_hbm.1) | copy-start | bytes 220
  2.3 0.7 %copy-start.2 = (s32[5]{0:T(128)S(1)}, s32[5]{0:T(128)}, u32[]{:S(2)}) copy-start(s32[5]{0:T(128)} %branch_hbm.1) | copy-start | bytes 64

commit v3 on v2

--- a/solution.py
+++ b/solution.py
@@ -51,6 +51,8 @@
     u,
     m,
     selves,
+    ends,
+    cross,
     hbuf,
     ubuf,
     mbuf,
@@ -162,7 +164,7 @@
     def send_h(i):
         return [
             remote(
-                x.at[i, :, 1 - side, pl.ds(BLK - side * BLK, BLK)],
+                ends.at[i, 1 - side],
                 hbuf.at[i, side],
                 h_send.at[i, side],
                 h_recv.at[i, side],
@@ -186,7 +188,7 @@
     def send_m(i):
         return [
             remote(
-                m.at[i],
+                cross.at[i, 1 - line],
                 mbuf.at[i, line],
                 m_send.at[i, line],
                 m_recv.at[i, line],
@@ -236,12 +238,22 @@
         selves[i, 0] = pack(value[:BLK, :BLK])
         selves[i, 1] = pack(value[BLK:, BLK:])
 
+    def pack_messages(i):
+        for atom in range(2):
+            lines = slice(atom * BLK, atom * BLK + BLK)
+            lanes = slice(BLK - atom * BLK, two - atom * BLK)
+            ends[i, atom] = beside(x[i, 0, atom, lines][:, lanes], x[i, 1, atom, lines][:, lanes])
+        for line in range(2):
+            cross[i, line, 0] = m[i]
+            cross[i, line, 1] = jnp.where(low_lanes, x[i, line, 0, 0:BLK], x[i, line, 1, BLK:two])
+
     def start_own(i):
         start(send_c(i))
         start(send_u(i))
         start(send_s(i))
 
     pack_selves(0, u[0])
+    pack_messages(0)
     pl.semaphore_wait(barrier, len(near_devices) + sum(size - 1 for size in sizes))
     start(send_h(0))
     start(send_m(0))
@@ -314,8 +326,9 @@
 
     def far_operands(i, line):
         above = ubuf[i, line]
-        edges = mbuf[i, line]
+        edges = mbuf[i, line, 0]
         turned = edges.T
+        diagonal = mbuf[i, line, 1].T
         pieces = (
             (0, 0, beside(unpack(cbuf[i, line, 0]), turned[:BLK])),
             (1, 0, beside(edges[:, :BLK], above[:BLK, :BLK])),
@@ -328,6 +341,11 @@
             high, low = split(value)
             far_hi[line, at * BLK : at * BLK + BLK, half * two : half * two + two] = high
             far_lo[line, at * BLK : at * BLK + BLK, half * two : half * two + two] = low
+        for side in range(2):
+            high, low = split(diagonal[side * BLK : side * BLK + BLK])
+            base = line * two + BLK - side * BLK
+            h_pair[side, 0:BLK, base : base + BLK] = high
+            h_pair[side, BLK:two, base : base + BLK] = low
 
     def far_part(line):
         both = dot(pair[:, x_lanes(line)], far_hi[line])
@@ -345,10 +363,11 @@
 
     def message_operands(i):
         for side in range(2):
+            high, low = split(hbuf[i, side])
             for line in range(2):
-                high, low = split(hbuf[i, side, line])
-                h_pair[side, 0:BLK, line * two : line * two + two] = high
-                h_pair[side, BLK:two, line * two : line * two + two] = low
+                base = line * two + side * BLK
+                h_pair[side, 0:BLK, base : base + BLK] = high[:, line * BLK : line * BLK + BLK]
+                h_pair[side, BLK:two, base : base + BLK] = low[:, line * BLK : line * BLK + BLK]
 
     def message_products():
         outer, edge = [], []
@@ -397,6 +416,11 @@
             for step in steps
         ]
 
+    def gather_stats():
+        sums = jnp.sum(stats[...], axis=1, keepdims=True)
+        lanes = lax.broadcasted_iota(jnp.int32, (8, two), 1)
+        return fold(jnp.where(lanes == s_iota, sums, 0.0))
+
     def reduce_begin(phase, value):
         reduced[phase, own[phase]] = value
         copies = reduce_copies(phase)
@@ -441,6 +465,7 @@
             m[i + 1] = value
 
         finish(i, sums, near_sum, emit_x, emit_m)
+        pack_messages(i + 1)
         start(send_h(i + 1))
         start(send_m(i + 1))
         return carry
@@ -449,7 +474,7 @@
 
     last = ITERS - 1
     add_stats(last)
-    copies0 = reduce_begin(0, stats[...])
+    copies0 = reduce_begin(0, gather_stats())
     own_operands(last)
     fresh = next_u(last)
     sums, near_sum = before_message(last)
@@ -484,8 +509,7 @@
     wait_send(copies0)
     wait_send(copies1)
     total = reduce_end(2, copies2)
-    for i in range(ITERS):
-        occupation_ref[i] = jnp.sum(total[i : i + 1]) / order
+    occupation_ref[...] = total / order
     wait_send(copies2)
 
 
@@ -494,18 +518,17 @@
     sizes = (rows // 2, max(cols // 4, 1), 2 * min(cols, 4))
     slots = max(sizes)
     vmem = pl.BlockSpec(memory_space=pltpu.VMEM)
-    smem = pl.BlockSpec(memory_space=pltpu.SMEM)
     hbm = pl.BlockSpec(memory_space=pltpu.HBM)
     dma = pltpu.SemaphoreType.DMA
     f32, bf16 = jnp.float32, jnp.bfloat16
-    return pl.pallas_call(
+    density, sums = pl.pallas_call(
         functools.partial(kernel, rows, cols, order),
         out_shape=(
             jax.ShapeDtypeStruct(initial.shape, jnp.float32),
-            jax.ShapeDtypeStruct((ITERS,), jnp.float32),
+            jax.ShapeDtypeStruct((1, 2 * BLK), jnp.float32),
         ),
         in_specs=[hbm, hbm, hbm],
-        out_specs=(vmem, smem),
+        out_specs=(vmem, vmem),
         scratch_shapes=[
             pltpu.SMEM(branch.shape, jnp.int32),
             pltpu.SMEM(pattern.shape, jnp.int32),
@@ -514,9 +537,11 @@
             pltpu.VMEM((ITERS, two, two), f32),
             pltpu.VMEM((ITERS, BLK, two), f32),
             pltpu.VMEM((ITERS, 2, BLK // 2, two), f32),
+            pltpu.VMEM((ITERS, 2, BLK, two), f32),
             pltpu.VMEM((ITERS, 2, 2, BLK, two), f32),
+            pltpu.VMEM((ITERS, 2, BLK, two), f32),
             pltpu.VMEM((ITERS, 2, two, two), f32),
-            pltpu.VMEM((ITERS, 2, BLK, two), f32),
+            pltpu.VMEM((ITERS, 2, 2, BLK, two), f32),
             pltpu.VMEM((ITERS, 2, BLK // 2, two), f32),
             pltpu.VMEM((ITERS, 2, 2, BLK // 2, two), f32),
             pltpu.VMEM((2, 2, two, two), f32),
@@ -529,7 +554,7 @@
             pltpu.VMEM((2, two, two), bf16),
             pltpu.VMEM((2, two, 2 * two), bf16),
             pltpu.VMEM((8, two), f32),
-            pltpu.VMEM((3, slots, 8, two), f32),
+            pltpu.VMEM((3, slots, 1, two), f32),
             dma((3,)),
             dma((ITERS, 2)),
             dma((ITERS, 2)),
@@ -545,10 +570,11 @@
             dma((3, slots)),
         ],
         compiler_params=pltpu.CompilerParams(
-            collective_id=0, has_side_effects=True, vmem_limit_bytes=32 * 1024 * 1024
+            collective_id=0, has_side_effects=True, vmem_limit_bytes=63 * 1024 * 1024
         ),
         cost_estimate=pl.CostEstimate(flops=1800000000, bytes_accessed=600000, transcendentals=0),
     )(branch, pattern, initial)
+    return density, sums[0, :ITERS]
 
 
 def solution(mesh):

time: 58.4 us -> 55.2 us (0.945)
  Pallas kernels: 54 us -> 51.5 us
  local copies, waits for them, and re-layouts: 3.54 us -> 2.83 us
    pallas_call x1, Pallas kernels: 54 us -> 51.5 us  [on_device(): pl.pallas_call(functools.partial(kernel, rows, cols, order), out_shape=(j...]
    unnamed x8 -> x3, local copies, waits for them, and re-layouts: 3.54 us -> 2.32 us
where the time goes in v3:
time: 55.2 us; the launch traced here: 55 us
  Pallas kernels  51.5 us (93%)
  local copies, waits for them, and re-layouts  2.83 us (5%)
  between operations  0.65 us (1%)
    pallas_call x1, Pallas kernels, on_device(): pl.pallas_call(functools.partial(kernel, rows, cols, order), out_shape=(j...  51.5 us
    unnamed x3, local copies, waits for them, and re-layouts  2.32 us

profile of v3, /device:TPU:1, one launch (start us, length us, event | category | flops | bytes accessed | tf_op | source)
XLA Modules:
  0.0 55.0 jit_solution(5913800377674885620)
XLA Ops:
  0.6 51.5 %shard_map.50 = (f32[1,2,64,576]{3,2,1,0:T(8,128)}, f32[1,128]{1,0:T(1,128)}) custom-call(s32[5]{0:T(128)} %branch_hbm.1, s32[1,2,9]{2,1,0:T(2,128)} %pattern_hbm.1, f32[1,2,64,576]{3,2,1,0:T(8,128)} %initial_hbm.1), custom_call_target="tpu_custom_call" | custom-call | flops 1800000000 | bytes 600000 | tf_op jit(solution)/shard_map/pallas_call | solution.py:524
  52.2 0.0 copy-start
  52.2 0.6 %copy-done = f32[1,128]{1,0:T(1,128)S(1)} copy-done((f32[1,128]{1,0:T(1,128)S(1)}, f32[1,128]{1,0:T(1,128)}, u32[]{:S(2)}) %copy-start) | copy-done | bytes 536
  52.8 0.5 slice_bitcast_fusion
  53.3 1.7 %copy.6 = f32[1,2,64,576]{3,2,1,0:T(8,128)} copy(f32[1,2,64,576]{3,2,1,0:T(8,128)} %get-tuple-element.8) | data formatting | bytes 589824
Async XLA Ops:
  52.2 0.6 %copy-start = (f32[1,128]{1,0:T(1,128)S(1)}, f32[1,128]{1,0:T(1,128)}, u32[]{:S(2)}) copy-start(f32[1,128]{1,0:T(1,128)} %get-tuple-element.5) | copy-start | bytes 1540

commit v4 on v3

--- a/solution.py
+++ b/solution.py
@@ -521,6 +521,9 @@
     hbm = pl.BlockSpec(memory_space=pltpu.HBM)
     dma = pltpu.SemaphoreType.DMA
     f32, bf16 = jnp.float32, jnp.bfloat16
+    initial, pattern, branch = (
+        pltpu.with_memory_space_constraint(value, pltpu.HBM) for value in (initial, pattern, branch)
+    )
     density, sums = pl.pallas_call(
         functools.partial(kernel, rows, cols, order),
         out_shape=(
@@ -570,7 +573,7 @@
             dma((3, slots)),
         ],
         compiler_params=pltpu.CompilerParams(
-            collective_id=0, has_side_effects=True, vmem_limit_bytes=63 * 1024 * 1024
+            collective_id=0, has_side_effects=True, vmem_limit_bytes=32 * 1024 * 1024
         ),
         cost_estimate=pl.CostEstimate(flops=1800000000, bytes_accessed=600000, transcendentals=0),
     )(branch, pattern, initial)

time: 55.2 us -> 52.8 us (0.957)
  local copies, waits for them, and re-layouts: 2.83 us -> 1.24 us
  Pallas kernels: 51.5 us -> 50.8 us
    unnamed x3 -> x1, local copies, waits for them, and re-layouts: 2.32 us -> 0.72 us
    pallas_call x1, Pallas kernels: 51.5 us -> 50.8 us  [on_device(): pl.pallas_call(functools.partial(kernel, rows, cols, order), out_shape=(j...]
where the time goes in v4:
time: 52.8 us; the launch traced here: 52.7 us
  Pallas kernels  50.8 us (96%)
  local copies, waits for them, and re-layouts  1.24 us (2%)
  between operations  0.64 us (1%)
    pallas_call x1, Pallas kernels, on_device(): pl.pallas_call(functools.partial(kernel, rows, cols, order), out_shape=(j...  50.8 us

profile of v4, /device:TPU:1, one launch (start us, length us, event | category | flops | bytes accessed | tf_op | source)
XLA Modules:
  0.0 52.7 jit_solution(16163592880680112985)
XLA Ops:
  0.6 50.8 %shard_map.50 = (f32[1,2,64,576]{3,2,1,0:T(8,128)S(1)}, f32[1,128]{1,0:T(1,128)S(1)}) custom-call(s32[5]{0:T(128)} %branch_hbm.1, s32[1,2,9]{2,1,0:T(2,128)} %pattern_hbm.1, f32[1,2,64,576]{3,2,1,0:T(8,128)} %initial_hbm.1), custom_call_target="tpu_custom_call" | custom-call | flops 1800000000 | bytes 600000 | tf_op jit(solution)/shard_map/pallas_call | solution.py:527
  51.4 0.5 slice_bitcast_fusion
  51.9 0.7 %copy.6 = f32[1,2,64,576]{3,2,1,0:T(8,128)} copy(f32[1,2,64,576]{3,2,1,0:T(8,128)S(1)} %get-tuple-element.8) | data formatting | bytes 589824

commit v5 on v4

--- a/solution.py
+++ b/solution.py
@@ -88,19 +88,11 @@
     north, south = lax.rem(row + rows - 1, rows), lax.rem(row + 1, rows)
     two = 2 * BLK
 
-    ys, zs, xs = rows // 2, max(cols // 4, 1), min(cols, 4)
-    y, core = row // 2, lax.rem(row, 2)
-    z, xx = col // xs, lax.rem(col, xs)
-
     def member(phase, index):
-        if phase == 0:
-            return (index * 2 + core, col)
-        if phase == 1:
-            return (row, index * xs + xx)
-        return (y * 2 + index // xs, z * xs + lax.rem(index, xs))
-
-    own = (y, z, core * xs + xx)
-    sizes = (ys, zs, 2 * xs)
+        return (index, col) if phase == 0 else (row, index)
+
+    own = (row, col)
+    sizes = (rows, cols)
 
     barrier = pltpu.get_barrier_semaphore()
     near_devices = [(row, west), (row, east)] + [
@@ -115,7 +107,7 @@
     ]
     for copy in inputs:
         copy.start()
-    for phase in range(3):
+    for phase in range(2):
         for step in range(1, sizes[phase]):
             device = member(phase, lax.rem(own[phase] + step, sizes[phase]))
             pl.semaphore_signal(barrier, inc=1, device_id=device, device_id_type=MESH)
@@ -238,11 +230,13 @@
         selves[i, 0] = pack(value[:BLK, :BLK])
         selves[i, 1] = pack(value[BLK:, BLK:])
 
-    def pack_messages(i):
+    def pack_ends(i):
         for atom in range(2):
             lines = slice(atom * BLK, atom * BLK + BLK)
             lanes = slice(BLK - atom * BLK, two - atom * BLK)
             ends[i, atom] = beside(x[i, 0, atom, lines][:, lanes], x[i, 1, atom, lines][:, lanes])
+
+    def pack_cross(i):
         for line in range(2):
             cross[i, line, 0] = m[i]
             cross[i, line, 1] = jnp.where(low_lanes, x[i, line, 0, 0:BLK], x[i, line, 1, BLK:two])
@@ -253,7 +247,8 @@
         start(send_s(i))
 
     pack_selves(0, u[0])
-    pack_messages(0)
+    pack_ends(0)
+    pack_cross(0)
     pl.semaphore_wait(barrier, len(near_devices) + sum(size - 1 for size in sizes))
     start(send_h(0))
     start(send_m(0))
@@ -369,11 +364,16 @@
                 h_pair[side, 0:BLK, base : base + BLK] = high[:, line * BLK : line * BLK + BLK]
                 h_pair[side, BLK:two, base : base + BLK] = low[:, line * BLK : line * BLK + BLK]
 
-    def message_products():
-        outer, edge = [], []
+    def outer_products():
+        outer = []
         for side in range(2):
             both = dot(left_side[side], h_pair[side])
             outer.append(both[:BLK] + both[BLK:])
+        return outer
+
+    def edge_products():
+        edge = []
+        for side in range(2):
             high = slice(side * BLK, side * BLK + BLK)
             low = slice(two + side * BLK, two + side * BLK + BLK)
             links = jnp.concatenate(
@@ -385,10 +385,10 @@
             )
             both = dot(links, h_pair[side], True)
             edge.append(both[:BLK, :BLK] + both[:BLK, BLK:] + both[BLK:, :BLK])
-        return outer, beside(edge[0], edge[1])
-
-    def finish(i, sums, near_sum, emit_x, emit_m):
-        outer, edge = message_products()
+        return beside(edge[0], edge[1])
+
+    def finish_x(i, sums, emit_x):
+        outer = outer_products()
         for line in range(2):
             for half in range(2):
                 square = sums[line][:, half * two : half * two + two]
@@ -400,8 +400,10 @@
                     low = low + extra
                 square = jnp.concatenate([top, low], axis=0)
                 emit_x(line, half, polynomial(i, x[i, line, half], square, mask_x[line, half]))
-        square = jnp.where(low_lanes, near_sum[:BLK], near_sum[BLK:]) + edge
-        emit_m(polynomial(i, m[i], square, mask_m[...]))
+
+    def next_m(i, near_sum):
+        square = jnp.where(low_lanes, near_sum[:BLK], near_sum[BLK:]) + edge_products()
+        return polynomial(i, m[i], square, mask_m[...])
 
     def reduce_copies(phase):
         steps = sorted(range(1, sizes[phase]), key=lambda step: -min(step, sizes[phase] - step))
@@ -434,11 +436,12 @@
             total = total + reduced[phase, index]
         return total
 
-    def before_message(i):
+    def before_message(i, between):
         sums = [own_part(line) for line in range(2)]
         side_operands()
         wait_recv(send_s(i))
         near_sum = near_part(i)
+        between()
         wait_recv(send_u(i))
         wait_recv(send_c(i))
         wait_recv(send_m(i))
@@ -454,19 +457,18 @@
         pack_selves(i + 1, fresh)
         start_own(i + 1)
         add_stats(i)
-        sums, near_sum = before_message(i)
+        sums, near_sum = before_message(i, lambda: None)
         wait_recv(send_h(i))
         message_operands(i)
 
         def emit_x(line, half, value):
             x[i + 1, line, half] = value
 
-        def emit_m(value):
-            m[i + 1] = value
-
-        finish(i, sums, near_sum, emit_x, emit_m)
-        pack_messages(i + 1)
+        finish_x(i, sums, emit_x)
+        pack_ends(i + 1)
         start(send_h(i + 1))
+        m[i + 1] = next_m(i, near_sum)
+        pack_cross(i + 1)
         start(send_m(i + 1))
         return carry
 
@@ -477,8 +479,12 @@
     copies0 = reduce_begin(0, gather_stats())
     own_operands(last)
     fresh = next_u(last)
-    sums, near_sum = before_message(last)
-    copies1 = reduce_begin(1, reduce_end(0, copies0))
+    copies1 = []
+
+    def second_phase():
+        copies1.extend(reduce_begin(1, reduce_end(0, copies0)))
+
+    sums, near_sum = before_message(last, second_phase)
     wait_recv(send_h(last))
     message_operands(last)
     parts = {}
@@ -486,19 +492,15 @@
     def keep_x(line, half, value):
         parts[line, half] = value
 
-    def keep_m(value):
-        parts["m"] = value
-
-    finish(last, sums, near_sum, keep_x, keep_m)
+    finish_x(last, sums, keep_x)
     for line in range(2):
         base = 6 * line * BLK
         a, b = parts[line, 0], parts[line, 1]
         density_ref[0, 0, :, base : base + 3 * BLK] = beside(a[:BLK], b[:BLK, :BLK])
         density_ref[0, 1, :, base : base + 3 * BLK] = beside(a[BLK:, BLK:], b[BLK:])
-    edges = parts["m"]
+    edges = next_m(last, near_sum)
     density_ref[0, 0, :, 3 * BLK : 6 * BLK] = beside(edges[:, :BLK], fresh[:BLK])
     density_ref[0, 1, :, 3 * BLK : 6 * BLK] = beside(fresh[BLK:], edges[:, BLK:])
-    copies2 = reduce_begin(2, reduce_end(1, copies1))
 
     def drain(i, carry):
         for copies in (send_h(i), send_m(i), send_u(i), send_s(i), send_c(i)):
@@ -507,16 +509,14 @@
 
     lax.fori_loop(0, ITERS, drain, 0)
     wait_send(copies0)
+    total = reduce_end(1, copies1)
+    occupation_ref[...] = total / order
     wait_send(copies1)
-    total = reduce_end(2, copies2)
-    occupation_ref[...] = total / order
-    wait_send(copies2)
 
 
 def on_device(rows, cols, order, initial, pattern, branch):
     two = 2 * BLK
-    sizes = (rows // 2, max(cols // 4, 1), 2 * min(cols, 4))
-    slots = max(sizes)
+    slots = max(rows, cols)
     vmem = pl.BlockSpec(memory_space=pltpu.VMEM)
     hbm = pl.BlockSpec(memory_space=pltpu.HBM)
     dma = pltpu.SemaphoreType.DMA
@@ -557,7 +557,7 @@
             pltpu.VMEM((2, two, two), bf16),
             pltpu.VMEM((2, two, 2 * two), bf16),
             pltpu.VMEM((8, two), f32),
-            pltpu.VMEM((3, slots, 1, two), f32),
+            pltpu.VMEM((2, slots, 1, two), f32),
             dma((3,)),
             dma((ITERS, 2)),
             dma((ITERS, 2)),
@@ -569,8 +569,8 @@
             dma((ITERS, 2)),
             dma((ITERS, 2, 2)),
             dma((ITERS, 2, 2)),
-            dma((3, slots)),
-            dma((3, slots)),
+            dma((2, slots)),
+            dma((2, slots)),
         ],
         compiler_params=pltpu.CompilerParams(
             collective_id=0, has_side_effects=True, vmem_limit_bytes=32 * 1024 * 1024

time: 52.8 us -> 51.6 us (0.977)
  Pallas kernels: 50.8 us -> 49.6 us
    pallas_call x1, Pallas kernels: 50.8 us -> 49.6 us  [on_device(): pl.pallas_call(functools.partial(kernel, rows, cols, order), out_shape=(j...]
where the time goes in v5:
time: 51.6 us; the launch traced here: 51.4 us
  Pallas kernels  49.6 us (96%)
  local copies, waits for them, and re-layouts  1.24 us (2%)
  between operations  0.64 us (1%)
    pallas_call x1, Pallas kernels, on_device(): pl.pallas_call(functools.partial(kernel, rows, cols, order), out_shape=(j...  49.6 us

profile of v5, /device:TPU:1, one launch (start us, length us, event | category | flops | bytes accessed | tf_op | source)
XLA Modules:
  0.0 51.4 jit_solution(9633283663053977323)
XLA Ops:
  0.6 49.6 %shard_map.50 = (f32[1,2,64,576]{3,2,1,0:T(8,128)S(1)}, f32[1,128]{1,0:T(1,128)S(1)}) custom-call(s32[5]{0:T(128)} %branch_hbm.1, s32[1,2,9]{2,1,0:T(2,128)} %pattern_hbm.1, f32[1,2,64,576]{3,2,1,0:T(8,128)} %initial_hbm.1), custom_call_target="tpu_custom_call" | custom-call | flops 1800000000 | bytes 600000 | tf_op jit(solution)/shard_map/pallas_call | solution.py:527
  50.2 0.5 slice_bitcast_fusion
  50.7 0.7 %copy.6 = f32[1,2,64,576]{3,2,1,0:T(8,128)} copy(f32[1,2,64,576]{3,2,1,0:T(8,128)S(1)} %get-tuple-element.8) | data formatting | bytes 589824

commit v6 on v5

--- a/solution.py
+++ b/solution.py
@@ -450,7 +450,7 @@
         sums = [sums[line] + far_part(line) for line in range(2)]
         return sums, near_sum
 
-    def body(i, carry):
+    def step(i, ahead):
         own_operands(i)
         fresh = next_u(i)
         u[i + 1] = fresh
@@ -465,18 +465,31 @@
             x[i + 1, line, half] = value
 
         finish_x(i, sums, emit_x)
-        pack_ends(i + 1)
-        start(send_h(i + 1))
-        m[i + 1] = next_m(i, near_sum)
+        if ahead is None:
+            pack_ends(i + 1)
+            start(send_h(i + 1))
+            m[i + 1] = next_m(i, near_sum)
+        else:
+            m[i + 1] = next_m(i, near_sum)
+            ahead()
+            pack_ends(i + 1)
+            start(send_h(i + 1))
         pack_cross(i + 1)
         start(send_m(i + 1))
+
+    def body(i, carry):
+        step(i, None)
         return carry
 
-    lax.fori_loop(0, ITERS - 1, body, 0)
-
     last = ITERS - 1
-    add_stats(last)
-    copies0 = reduce_begin(0, gather_stats())
+    copies0 = []
+
+    def first_phase():
+        add_stats(last)
+        copies0.extend(reduce_begin(0, gather_stats()))
+
+    lax.fori_loop(0, ITERS - 2, body, 0)
+    step(ITERS - 2, first_phase)
     own_operands(last)
     fresh = next_u(last)
     copies1 = []

time: 51.6 us -> 51.3 us (level)
  no operation moved by 1% of the time
where the time goes in v6:
time: 51.3 us; the launch traced here: 51.2 us
  Pallas kernels  49.3 us (96%)
  local copies, waits for them, and re-layouts  1.24 us (2%)
  between operations  0.64 us (1%)
    pallas_call x1, Pallas kernels, on_device(): pl.pallas_call(functools.partial(kernel, rows, cols, order), out_shape=(j...  49.3 us

profile of v6, /device:TPU:1, one launch (start us, length us, event | category | flops | bytes accessed | tf_op | source)
XLA Modules:
  0.0 51.2 jit_solution(18386083082260795470)
XLA Ops:
  0.6 49.3 %shard_map.50 = (f32[1,2,64,576]{3,2,1,0:T(8,128)S(1)}, f32[1,128]{1,0:T(1,128)S(1)}) custom-call(s32[5]{0:T(128)} %branch_hbm.1, s32[1,2,9]{2,1,0:T(2,128)} %pattern_hbm.1, f32[1,2,64,576]{3,2,1,0:T(8,128)} %initial_hbm.1), custom_call_target="tpu_custom_call" | custom-call | flops 1800000000 | bytes 600000 | tf_op jit(solution)/shard_map/pallas_call | solution.py:540
  49.9 0.5 %slice_bitcast_fusion = f32[5]{0:T(128)} fusion(f32[1,128]{1,0:T(1,128)S(1)} %get-tuple-element.5), kind=kLoop, calls=%fused_computation | loop fusion | bytes 40 | tf_op jit(solution)/shard_map/squeeze | solution.py:593
  50.4 0.7 %copy.6 = f32[1,2,64,576]{3,2,1,0:T(8,128)} copy(f32[1,2,64,576]{3,2,1,0:T(8,128)S(1)} %get-tuple-element.8) | data formatting | bytes 589824
